TPU v7x, 512 devices: a whole 4x8x8 slice. The times are simulated.
512 devices in a mesh: lat: 16 (over y_hi, z), lon: 32 (over x, y_lo, core).
Axes of the slice: x: 4, y: 8 (y_hi: 2, y_lo: 4; y = y_hi * 4 + y_lo), z: 8, core: 2. Of those that a mesh axis runs over, the one named last changes fastest.
Arguments:
- tokens: bfloat16 [4, 96, 1152, 512], P(None, 'lat', 'lon'), may hold values from -6 to 6
- gain_attn: float32 [512], replicated, may hold values from 0.1 to 1.9
- gain_mlp: float32 [512], replicated, may hold values from 0.1 to 1.9
- w_qkv: bfloat16 [512, 1536], P('lon'), may hold values from -1 to 1
- w_proj: bfloat16 [512, 512], P('lon'), may hold values from -0.25 to 0.25
- w_up: bfloat16 [512, 2048], P('lon'), may hold values from -0.25 to 0.25
- w_down: bfloat16 [2048, 512], P('lon'), may hold values from -0.125 to 0.125
Outputs:
- block_out: bfloat16 [4, 96, 1152, 512], P(None, 'lat', 'lon')
All inputs are finite; a program needn't handle non-finite values.
Results may differ from a plain program's by a relative error of at most 0.0055.
Values may be sent and summed in bfloat16 or wider, within the bound.
No kernel may reach another device: no remote copies, remote signals or barrier semaphores. Data moves between devices by JAX's collectives and lax.ppermute only.
A program may use at most 128 MiB of HBM per device.

v0:
```python
import jax
import jax.numpy as jnp
from jax import lax
from jax.sharding import PartitionSpec as P

HEADS = 8
WIN_LEV = 2
WIN_LAT = 6
WIN_LON = 12


def from_behind(shard, axis, by):
    devices = lax.axis_size(axis)
    return lax.ppermute(shard, axis, [(i, (i + by) % devices) for i in range(devices)])


def layer_norm(values, gain):
    values = values.astype(jnp.float32)
    center = values - jnp.mean(values, axis=-1, keepdims=True)
    spread = jnp.mean(center * center, axis=-1, keepdims=True)
    return center * lax.rsqrt(spread + 1e-05) * gain


def attend(region, lat_labels, gain_attn, full_qkv):
    levels, rows, columns, features = region.shape
    head_size = features // HEADS
    normed = layer_norm(region, gain_attn).astype(jnp.bfloat16)
    projected = jnp.dot(
        normed.reshape(-1, features), full_qkv, preferred_element_type=jnp.float32
    ).astype(jnp.bfloat16)
    projected = projected.reshape(
        levels // WIN_LEV,
        WIN_LEV,
        rows // WIN_LAT,
        WIN_LAT,
        columns // WIN_LON,
        WIN_LON,
        3,
        HEADS,
        head_size,
    )
    projected = projected.transpose(0, 2, 4, 6, 7, 1, 3, 5, 8)
    windows = levels // WIN_LEV * (rows // WIN_LAT) * (columns // WIN_LON)
    span = WIN_LEV * WIN_LAT * WIN_LON
    projected = projected.reshape(windows, 3, HEADS, span, head_size)
    query = projected[:, 0]
    keys = projected[:, 1]
    values = projected[:, 2]
    level_pos = jnp.arange(levels)
    level_labels = jnp.where(
        level_pos < levels - WIN_LEV, 0, jnp.where(level_pos < levels - WIN_LEV // 2, 1, 2)
    )
    labels = level_labels[:, None] * 3 + lat_labels[None, :]
    labels = jnp.broadcast_to(labels[:, :, None], (levels, rows, columns))
    labels = labels.reshape(
        levels // WIN_LEV, WIN_LEV, rows // WIN_LAT, WIN_LAT, columns // WIN_LON, WIN_LON
    )
    labels = labels.transpose(0, 2, 4, 1, 3, 5).reshape(windows, span)
    allowed = labels[:, :, None] == labels[:, None, :]
    scores = jnp.einsum(
        "whqd,whkd->whqk", query, keys, preferred_element_type=jnp.float32
    ) * head_size ** (-0.5)
    scores = jnp.where(allowed[:, None], scores, -jnp.inf)
    scores = scores - jnp.max(scores, axis=-1, keepdims=True)
    expo = jnp.exp(scores)
    probability = (expo / jnp.sum(expo, axis=-1, keepdims=True)).astype(jnp.bfloat16)
    attended = jnp.einsum(
        "whqk,whkd->whqd", probability, values, preferred_element_type=jnp.float32
    ).astype(jnp.bfloat16)
    attended = attended.reshape(
        levels // WIN_LEV,
        rows // WIN_LAT,
        columns // WIN_LON,
        HEADS,
        WIN_LEV,
        WIN_LAT,
        WIN_LON,
        head_size,
    )
    attended = attended.transpose(0, 4, 1, 5, 2, 6, 3, 7)
    return attended.reshape(-1, features)


def finish(residual_in, attended, full_proj, gain_mlp, up_apply, down_apply):
    residual = residual_in.astype(jnp.float32) + jnp.dot(
        attended, full_proj, preferred_element_type=jnp.float32
    )
    normed = layer_norm(residual, gain_mlp).astype(jnp.bfloat16)
    hidden = jax.nn.gelu(up_apply(normed), approximate=False).astype(jnp.bfloat16)
    return (residual + down_apply(hidden)).astype(jnp.bfloat16)


def band_labels(region_rows, rows):
    lat_index = lax.axis_index("lat")
    total_rows = rows * lax.axis_size("lat")
    position = jnp.mod(
        lat_index * rows - 2 * (WIN_LAT // 2) + jnp.arange(region_rows, dtype=jnp.int32), total_rows
    )
    return jnp.where(
        position < total_rows - WIN_LAT, 0, jnp.where(position < total_rows - WIN_LAT // 2, 1, 2)
    )


def body(tokens, gain_attn, gain_mlp, w_qkv, w_proj, w_up, w_down):
    full_qkv, full_proj, full_up, full_down = (
        lax.all_gather(w_qkv, "lon", axis=0, tiled=True),
        lax.all_gather(w_proj, "lon", axis=0, tiled=True),
        lax.all_gather(w_up, "lon", axis=0, tiled=True),
        lax.all_gather(w_down, "lon", axis=0, tiled=True),
    )

    def up_apply(normed):
        return jnp.dot(normed, full_up, preferred_element_type=jnp.float32)

    def down_apply(hidden):
        return jnp.dot(hidden, full_down, preferred_element_type=jnp.float32)

    levels, rows, columns, features = tokens.shape
    half_rows = WIN_LAT // 2
    half_cols = WIN_LON // 2
    rolled = jnp.roll(tokens, -(WIN_LEV // 2), axis=0)
    west_rim = from_behind(rolled[:, :, columns - half_cols :, :], "lon", 1)
    widened = jnp.concatenate([west_rim, rolled[:, :, : columns - half_cols, :]], axis=2)
    north_rim = from_behind(widened[:, rows - half_rows :], "lat", 1)
    region = jnp.concatenate([north_rim, widened[:, : rows - half_rows]], axis=1)
    attended = attend(region, band_labels(rows, rows), gain_attn, full_qkv)
    result = finish(
        region.reshape(-1, features), attended, full_proj, gain_mlp, up_apply, down_apply
    )
    result = result.reshape(region.shape)
    south_back = from_behind(result[:, :half_rows], "lat", -1)
    row_done = jnp.concatenate([result[:, half_rows:], south_back], axis=1)
    east_back = from_behind(row_done[:, :, :half_cols], "lon", -1)
    owned = jnp.concatenate([row_done[:, :, half_cols:], east_back], axis=2)
    return jnp.roll(owned, WIN_LEV // 2, axis=0)


def solution(mesh):
    return jax.shard_map(
        body,
        mesh=mesh,
        in_specs=(
            P(None, "lat", "lon", None),
            P(),
            P(),
            P("lon", None),
            P("lon", None),
            P("lon", None),
            P("lon", None),
        ),
        out_specs=P(None, "lat", "lon", None),
        check_vma=False,
    )
```

profile of v0, /device:TPU:1, one launch (start us, length us, event | category | flops | bytes accessed | tf_op | source)
XLA Modules:
  0.0 284.3 jit_solution(18028926523285603713)
XLA Ops:
  8.1 1.6 slice.49
  9.7 1.5 slice.50
  11.3 4.6 %collective-permute-start = (bf16[4,6,6,512]{3,0,2,1:T(4,128)(2,1)S(1)}, bf16[4,6,6,512]{3,0,2,1:T(4,128)(2,1)S(1)}, u32[]{:S(2)}, u32[]{:S(2)}) collective-permute-start(bf16[4,6,6,512]{3,0,2,1:T(4,128)(2,1)S(1)} %pad_maximum_fusion.4), channel_id=1, source_target_pairs={{0,1},{1,2},{2,3},{3,4},{4,5},{5,6},{6,7},{7,8},{8,9},{9,10},{10,1... | collective-permute-start | bytes 442376 | tf_op jit(solution)/shard_map/ppermute | solution.py:14
  16.3 4.7 %collective-permute-done = bf16[4,6,6,512]{3,0,2,1:T(4,128)(2,1)S(1)} collective-permute-done((bf16[4,6,6,512]{3,0,2,1:T(4,128)(2,1)S(1)}, bf16[4,6,6,512]{3,0,2,1:T(4,128)(2,1)S(1)}, u32[]{:S(2)}, u32[]{:S(2)}) %collective-permute-start) | collective-permute-done | bytes 147488 | tf_op jit(solution)/shard_map/ppermute | solution.py:14
  21.0 0.8 fusion.28
  22.1 1.9 collective-permute-start.1
  24.1 0.9 broadcast_compare_fusion
  25.0 50.5 %all_gather.13 = bf16[512,512]{1,0:T(8,128)(2,1)} all-gather(bf16[16,512]{1,0:T(8,128)(2,1)S(1)} %copy-done.2), channel_id=1, replica_groups=mesh['lat'=16,'lon'=32] {'lon'}, dimensions={0}, use_global_device_ids=true | all-gather | bytes 540672 | tf_op jit(solution)/shard_map/all_gather | solution.py:107
  76.1 0.9 multiply_reduce_fusion.1
  78.3 1.4 reshape.127
  79.8 3.5 %convolution_convert_fusion = bf16[864,1536]{1,0:T(8,128)(2,1)S(1)} fusion(bf16[512,1536]{1,0:T(8,128)(2,1)} %all-gather.4.cloned.1.call-done, f32[864,512]{1,0:T(8,128)} %reshape.127, f32[512]{0:T(512)S(1)} %copy-done.3, f32[864]{0:T(1024)S(1)} %rsqrt.20, f32[864]{0:T(1024)S(1)} %div.23), kind=kOutput, calls=%fused_computation.29 | convolution fusion | flops 1362051072 | bytes 6005504 | tf_op jit(solution)/shard_map/dot_general | solution.py:28
  83.4 4.8 %reshape.122 = bf16[2,2,1,6,3,12,3,8,64]{8,7,6,5,4,3,1,0,2:T(8,128)(2,1)} reshape(bf16[864,1536]{1,0:T(8,128)(2,1)S(1)} %convolution_convert_fusion) | data formatting | bytes 5308416 | tf_op jit(solution)/shard_map/reshape | solution.py:31
  88.2 4.0 %copy.40 = bf16[2,2,1,6,3,12,3,8,64]{8,7,5,3,1,6,4,0,2:T(8,128)(2,1)S(1)} copy(bf16[2,2,1,6,3,12,3,8,64]{8,7,6,5,4,3,1,0,2:T(8,128)(2,1)} %reshape.122) | data formatting | bytes 5308416 | tf_op jit(solution)/shard_map/reshape | solution.py:31
  92.2 1.6 fusion.73
  93.9 3.8 %copy.50 = bf16[6,1,8,144,64]{3,4,2,0,1:T(8,128)(2,1)} copy(bf16[6,1,8,144,64]{4,2,3,1,0:T(8,128)(2,1)} %get-tuple-element.6) | data formatting | bytes 1769472
  97.7 2.4 copy.51
  100.1 1.2 copy.49
  101.3 3.1 %fusion.22 = f32[6,8,144,144]{2,3,1,0:T(8,128)S(1)} fusion(bf16[6,1,8,144,64]{3,4,2,0,1:T(8,128)(2,1)} %copy.51, bf16[6,1,8,144,64]{3,4,2,0,1:T(8,128)(2,1)} %copy.50), kind=kOutput, calls=%fused_computation.38 | convolution fusion | flops 127401984 | bytes 5750784 | tf_op jit(solution)/shard_map/whqd,whkd->whqk/dot_general | solution.py:60
  104.4 2.4 fusion.76
  106.9 2.0 fusion.20
  108.8 2.9 %copy.45 = bf16[6,8,144,64]{3,1,2,0:T(8,128)(2,1)S(1)} copy(bf16[6,8,144,64]{2,3,1,0:T(8,128)(2,1)} %fusion.20) | data formatting | bytes 1769472 | tf_op jit(solution)/shard_map/convert_element_type | solution.py:69
  111.8 1.4 copy.46
  113.2 3.7 %reshape.125 = bf16[864,512]{1,0:T(8,128)(2,1)} reshape(bf16[2,2,1,6,3,12,8,64]{7,6,5,4,3,1,0,2:T(8,128)(2,1)} %copy.46) | data formatting | bytes 1769472 | tf_op jit(solution)/shard_map/reshape | solution.py:81
  116.8 2.0 fusion.77
  119.3 36.1 %all-gather.6.cloned.1.call-done = bf16[512,2048]{1,0:T(8,128)(2,1)} async-done(((bf16[16,2048]{1,0:T(8,128)(2,1)}), bf16[512,2048]{1,0:T(8,128)(2,1)}) %all-gather.6.cloned.1.call-update) | async-done | bytes 2097168 | tf_op jit(solution)/shard_map/all_gather | solution.py:108
  155.4 64.0 %all-gather.8.cloned.1.call-done = bf16[2048,512]{1,0:T(8,128)(2,1)} async-done(((bf16[64,512]{1,0:T(8,128)(2,1)}), bf16[2048,512]{1,0:T(8,128)(2,1)}) %all-gather.8.cloned.1.call-update) | async-done | bytes 2097168 | tf_op jit(solution)/shard_map/all_gather | solution.py:109
  219.4 19.4 %add_convert_fusion = bf16[864,512]{1,0:T(8,128)(2,1)S(1)} fusion(f32[864,512]{1,0:T(8,128)S(1)} %get-tuple-element.15, bf16[2048,512]{1,0:T(8,128)(2,1)} %all-gather.8.cloned.1.call-done, bf16[512,2048]{1,0:T(8,128)(2,1)} %all-gather.6.cloned.1.call-done, f32[512]{0:T(512)S(1)} %copy-done.4, f32[864]{0:T(1024)S(1)} %add_rsqrt_fusion.1, ...), kind=kOutput, calls=%fused_computation.31 | convolution fusion | flops 3741548544 | bytes 6857472 | tf_op jit(solution)/shard_map/dot_general | solution.py:116
  239.1 9.2 %collective-permute-start.2 = (bf16[4,3,36,512]{3,2,1,0:T(8,128)(2,1)S(1)}, bf16[4,3,36,512]{3,2,1,0:T(8,128)(2,1)S(1)}, u32[]{:S(2)}, u32[]{:S(2)}) collective-permute-start(bf16[4,3,36,512]{3,2,1,0:T(8,128)(2,1)S(1)} %get-tuple-element.9), channel_id=1, source_target_pairs={{0,480},{32,0},{64,32},{96,64},{128,96},{160,128},{192,160},{224,1... | collective-permute-start | bytes 1327112 | tf_op jit(solution)/shard_map/ppermute | solution.py:14
  248.3 17.2 %collective-permute-done.2 = bf16[4,3,36,512]{3,2,1,0:T(8,128)(2,1)S(1)} collective-permute-done((bf16[4,3,36,512]{3,2,1,0:T(8,128)(2,1)S(1)}, bf16[4,3,36,512]{3,2,1,0:T(8,128)(2,1)S(1)}, u32[]{:S(2)}, u32[]{:S(2)}) %collective-permute-start.2) | collective-permute-done | bytes 442400 | tf_op jit(solution)/shard_map/ppermute | solution.py:14
  265.5 2.8 collective-permute-start.3
  268.5 7.5 %collective-permute-done.3 = bf16[4,6,6,512]{3,2,1,0:T(8,128)(2,1)S(1)} collective-permute-done((bf16[4,6,6,512]{3,2,1,0:T(8,128)(2,1)S(1)}, bf16[4,6,6,512]{3,2,1,0:T(8,128)(2,1)S(1)}, u32[]{:S(2)}, u32[]{:S(2)}) %collective-permute-start.3) | collective-permute-done | bytes 147488 | tf_op jit(solution)/shard_map/ppermute | solution.py:14
  276.2 1.6 copy.47
  (42 shorter events, 5.4 us)
Async XLA Ops:
  6.5 18.4 %copy-start.2 = (bf16[16,512]{1,0:T(8,128)(2,1)S(1)}, bf16[16,512]{1,0:T(8,128)(2,1)}, u32[]{:S(2)}) copy-start(bf16[16,512]{1,0:T(8,128)(2,1)} %param.11) | copy-start | bytes 49156
  6.5 73.3 %all-gather.4.cloned.1.call-start = ((), (), s32[]{:S(2)}) async-start(), calls=%async_computation | async-start | bytes 1622016 | tf_op jit(solution)/shard_map/all_gather | solution.py:106
  7.3 148.1 %all-gather.6.cloned.1.call-start = ((), (), s32[]{:S(2)}) async-start(), calls=%async_computation.1 | async-start | bytes 2162688 | tf_op jit(solution)/shard_map/all_gather | solution.py:108
  8.0 211.4 %all-gather.8.cloned.1.call-start = ((), (), s32[]{:S(2)}) async-start(), calls=%async_computation.2 | async-start | bytes 2162688 | tf_op jit(solution)/shard_map/all_gather | solution.py:109
  11.3 9.6 %collective-permute-start = (bf16[4,6,6,512]{3,0,2,1:T(4,128)(2,1)S(1)}, bf16[4,6,6,512]{3,0,2,1:T(4,128)(2,1)S(1)}, u32[]{:S(2)}, u32[]{:S(2)}) collective-permute-start(bf16[4,6,6,512]{3,0,2,1:T(4,128)(2,1)S(1)} %pad_maximum_fusion.4), channel_id=1, source_target_pairs={{0,1},{1,2},{2,3},{3,4},{4,5},{5,6},{6,7},{7,8},{8,9},{9,10},{10,1... | collective-permute-start | bytes 442376 | tf_op jit(solution)/shard_map/ppermute | solution.py:14
  22.1 57.7 %copy-start.3 = (f32[512]{0:T(512)S(1)}, f32[512]{0:T(512)}, u32[]{:S(2)}) copy-start(f32[512]{0:T(512)} %param.8) | copy-start | bytes 6148
  22.1 53.3 %collective-permute-start.1 = (bf16[4,3,36,512]{3,0,2,1:T(4,128)(2,1)S(1)}, bf16[4,3,36,512]{3,0,2,1:T(4,128)(2,1)S(1)}, u32[]{:S(2)}, u32[]{:S(2)}) collective-permute-start(bf16[4,3,36,512]{3,0,2,1:T(4,128)(2,1)S(1)} %get-tuple-element.10), channel_id=1, source_target_pairs={{0,32},{32,64},{64,96},{96,128},{128,160},{160,192},{192,224},{224... | collective-permute-start | bytes 1327112 | tf_op jit(solution)/shard_map/ppermute | solution.py:14
  101.3 3.1 %copy-start.1 = (pred[6,144,144]{1,2,0:T(8,128)(4,1)S(1)}, pred[6,144,144]{1,2,0:T(8,128)(4,1)}, u32[]{:S(2)}) copy-start(pred[6,144,144]{1,2,0:T(8,128)(4,1)} %broadcast_compare_fusion) | copy-start | bytes 373252
  108.8 8.0 %copy-start = (f32[864,512]{1,0:T(8,128)S(1)}, f32[864,512]{1,0:T(8,128)}, u32[]{:S(2)}) copy-start(f32[864,512]{1,0:T(8,128)} %reshape.127) | copy-start | bytes 5308420
  111.8 107.6 %copy-start.4 = (f32[512]{0:T(512)S(1)}, f32[512]{0:T(512)}, u32[]{:S(2)}) copy-start(f32[512]{0:T(512)} %param.9) | copy-start | bytes 6148
  239.1 26.4 %collective-permute-start.2 = (bf16[4,3,36,512]{3,2,1,0:T(8,128)(2,1)S(1)}, bf16[4,3,36,512]{3,2,1,0:T(8,128)(2,1)S(1)}, u32[]{:S(2)}, u32[]{:S(2)}) collective-permute-start(bf16[4,3,36,512]{3,2,1,0:T(8,128)(2,1)S(1)} %get-tuple-element.9), channel_id=1, source_target_pairs={{0,480},{32,0},{64,32},{96,64},{128,96},{160,128},{192,160},{224,1... | collective-permute-start | bytes 1327112 | tf_op jit(solution)/shard_map/ppermute | solution.py:14
  265.5 10.5 %collective-permute-start.3 = (bf16[4,6,6,512]{3,2,1,0:T(8,128)(2,1)S(1)}, bf16[4,6,6,512]{3,2,1,0:T(8,128)(2,1)S(1)}, u32[]{:S(2)}, u32[]{:S(2)}) collective-permute-start(bf16[4,6,6,512]{3,2,1,0:T(8,128)(2,1)S(1)} %pad_maximum_fusion.3), channel_id=1, source_target_pairs={{0,31},{1,0},{2,1},{3,2},{4,3},{5,4},{6,5},{7,6},{8,7},{9,8},{10,9... | collective-permute-start | bytes 442376 | tf_op jit(solution)/shard_map/ppermute | solution.py:14
Sparse Core Ops, SparseCore 0:
  9.5 68.3 all-gather.3
  80.0 75.3 all-gather.5
  157.5 61.8 all-gather.7
where the time goes:
time: 285 us; the launch traced here: 284 us
  waiting for transfers between devices  131 us (46%)
  blocking collectives  50.5 us (18%)
  local copies, waits for them, and re-layouts  33.7 us (12%)
  matrix products  30 us (11%)
  starting transfers between devices  18.6 us (7%)
  between operations  13.4 us (5%)
  other arithmetic  7.14 us (3%)
    all_gather x1, waiting for transfers between devices, body(): lax.all_gather(w_down, 'lon', axis=0, tiled=True)  64 us
    all_gather x1, blocking collectives, body(): lax.all_gather(w_proj, 'lon', axis=0, tiled=True)  50.5 us
    all_gather x1, waiting for transfers between devices, body(): lax.all_gather(w_up, 'lon', axis=0, tiled=True)  36.1 us
    ppermute x4, waiting for transfers between devices, from_behind(): lax.ppermute(shard, axis, [(i, (i + by) % devices) for i in range(devices)])  29.4 us
    dot_general x1, matrix products, down_apply(): return jnp.dot(hidden, full_down, preferred_element_type=jnp.float32)  19.4 us
    ppermute x4, starting transfers between devices, from_behind(): lax.ppermute(shard, axis, [(i, (i + by) % devices) for i in range(devices)])  18.5 us
    reshape x2, local copies, waits for them, and re-layouts, attend(): projected.reshape(levels // WIN_LEV, WIN_LEV, rows // WIN_LAT, WIN_LAT, c...  8.85 us
    unnamed x13, local copies, waits for them, and re-layouts  7.44 us
  transfers between devices with their start and end apart: 7, of which 5 were waited for; matrix products, arithmetic and copies ran while one was open for 17% of the time, Pallas kernels for 0%

commit v1 on v0

v1 whole, which is shorter than its diff:
```python
import functools

import jax
import jax.numpy as jnp
from jax import lax
from jax.experimental import pallas as pl
from jax.experimental.pallas import tpu as pltpu
from jax.sharding import Mesh
from jax.sharding import PartitionSpec as P

BF16 = jnp.bfloat16
F32 = jnp.float32
LEV, ROWS, COLS, D = 4, 6, 36, 512
HALF, RIM = 3, 6
REG = ROWS + 2 * HALF
SLOT = 16
WINS = 4
PAD = 40
FLAT = LEV * ROWS * PAD
FF = 2048
QKV = 3 * D
REST = D + FF + 4 * D
OFFSETS = (0, 3, 1, 2)
VMEM = 56 * 1024 * 1024


def norm(values, gain):
    center = values - jnp.mean(values, axis=-1, keepdims=True)
    spread = jnp.mean(center * center, axis=-1, keepdims=True)
    return center * lax.rsqrt(spread + 1e-05) * gain


def shard_row(pos, mine, outer, inner):
    x, y, core = pos
    owner = core if mine else 1 - core
    first = owner == 0
    a, b = OFFSETS[outer], OFFSETS[inner]
    sx = lax.rem(x + jnp.where(first, a, b), 4)
    sy = lax.rem(y + jnp.where(first, b, a), 4)
    return sx * 8 + sy * 2 + owner


def pieces_of(refs):
    own, other = refs[:4], refs[4:]
    result = [(True, o, i, own[o].at[i]) for o in range(4) for i in range(4)]
    per = 4 // len(other)
    for o in range(4):
        for i in range(4):
            result.append((False, o, i, other[o // per].at[(o % per) * 4 + i]))
    return result


def place_tokens(stage, row, gain, main, west, east, xn_ref, dst):
    stage[row, 64:100, :] = norm(main.astype(F32), gain)
    stage[row, 0:RIM, :] = norm(west.astype(F32), gain)
    stage[row, 54:60, :] = norm(east.astype(F32), gain)
    stage[row, 6:12, :] = stage[row, 64:70, :]
    stage[row, 16:28, :] = stage[row, 70:82, :]
    stage[row, 32:44, :] = stage[row, 82:94, :]
    stage[row, 48:54, :] = stage[row, 94:100, :]
    xn_ref[dst] = stage[row, 0:64, :].reshape(WINS, SLOT, D).astype(BF16)


def attn_kernel(position, n_w, gain_ref, tok_ref, north_ref, south_ref, west_ref, east_ref, *refs):
    w_refs = refs[:n_w]
    out_ref, w_ref, stage, xn_ref, q_ref, kv_ref, nat_ref, sem = refs[n_w:]
    pos, band = position()
    copies = []
    for mine, o, i, src in pieces_of(w_refs):
        at = pl.multiple_of(shard_row(pos, mine, o, i) * 16, 16)
        copies.append(pltpu.make_async_copy(src, w_ref.at[pl.ds(at, 16), :], sem))
    for c in copies:
        c.start()

    gain = gain_ref[...]
    for r in range(REG):
        for s in range(WINS):
            stage[r, 16 * s + 8 : 16 * s + 16, :] = jnp.zeros((8, D), F32)

    def place(lev, _):
        for r in range(REG):
            if r < HALF:
                main = north_ref[lev, r]
            elif r < HALF + ROWS:
                main = tok_ref[lev, r - HALF]
            else:
                main = south_ref[lev, r - HALF - ROWS]
            place_tokens(
                stage, r, gain, main, west_ref[lev, r], east_ref[lev, r], xn_ref, lev * REG + r
            )
        return 0

    lax.fori_loop(0, LEV, place, 0)

    for c in copies:
        c.wait()

    def project(lev, _):
        rows = xn_ref[pl.ds(lev * REG, REG)].reshape(REG * WINS * SLOT, D)
        for part in range(2):
            kv = jnp.dot(
                rows, w_ref[:, D * (part + 1) : D * (part + 2)], preferred_element_type=F32
            ).astype(BF16)
            kv_ref[pl.ds(lev * REG, REG), :, :, D * part : D * (part + 1)] = kv.reshape(
                REG, WINS, SLOT, D
            )
        mine = xn_ref[pl.ds(lev * REG + HALF, ROWS)].reshape(ROWS * WINS * SLOT, D)
        q = jnp.dot(mine, w_ref[:, 0:D], preferred_element_type=F32).astype(BF16)
        q_ref[pl.ds(lev * ROWS, ROWS)] = (q * jnp.asarray(0.125, BF16)).reshape(ROWS, WINS, SLOT, D)
        return 0

    lax.fori_loop(0, LEV, project, 0)

    lane = lax.broadcasted_iota(jnp.int32, (1, 256), 1) // 64

    def window(h, j, levels, half):
        feats = slice(256 * half, 256 * half + 256)
        vals = slice(D + 256 * half, D + 256 * half + 256)
        n_q, n_k = len(levels) * HALF * SLOT, len(levels) * ROWS * SLOT
        q = jnp.concatenate(
            [q_ref[pl.ds(lv * ROWS + HALF * h, HALF), j, :, feats] for lv in levels], axis=0
        ).reshape(n_q, 256)
        k = jnp.concatenate(
            [kv_ref[pl.ds(lv * REG + ROWS * h, ROWS), j, :, feats] for lv in levels], axis=0
        ).reshape(n_k, 256)
        v = jnp.concatenate(
            [kv_ref[pl.ds(lv * REG + ROWS * h, ROWS), j, :, vals] for lv in levels], axis=0
        ).reshape(n_k, 256)
        key = lax.broadcasted_iota(jnp.int32, (1, n_k), 1)
        key_row = lax.rem(key // SLOT, ROWS)
        first_row = jnp.where(jnp.logical_and(h == 0, band == 0), HALF, 0)
        last_row = jnp.where(jnp.logical_and(h == 1, band == 15), HALF, ROWS)
        bias = jnp.where(lax.rem(key, SLOT) >= 2 * RIM, -jnp.inf, 0.0)
        bias = jnp.where(key_row < first_row, -jnp.inf, bias)
        bias = jnp.where(key_row >= last_row, -jnp.inf, bias)
        packed = jnp.concatenate(
            [jnp.where(lane == hh, q, jnp.zeros_like(q)) for hh in range(4)], axis=0
        )
        s = lax.dot_general(packed, k, (((1,), (1,)), ((), ())), preferred_element_type=F32)
        s = s + bias
        p = jnp.exp(s - jnp.max(s, axis=-1, keepdims=True))
        total = jnp.sum(p, axis=-1, keepdims=True)
        o = jnp.dot(p.astype(BF16), v, preferred_element_type=F32)
        o = o * (1.0 / total)
        result = o[0:n_q]
        for hh in range(1, 4):
            result = jnp.where(lane == hh, o[hh * n_q : (hh + 1) * n_q], result)
        return result.reshape(len(levels), HALF, SLOT, 256)

    starts = (0, 6, 18, 30)

    def attend(h, _):
        for j in range(WINS):
            skip, count = (RIM, RIM) if j == 0 else (0, RIM) if j == 3 else (0, 2 * RIM)
            for levels in ((1, 2), (0,), (3,)):
                for half in range(2):
                    got = window(h, j, levels, half)
                    for n, lv in enumerate(levels):
                        for r in range(HALF):
                            row = (lv * ROWS + HALF * h + r) * PAD
                            row = pl.multiple_of(row, 8)
                            block = nat_ref.at[pl.ds(row, PAD), 256 * half : 256 * half + 256]
                            block[starts[j] : starts[j] + count, :] = got[n, r, skip : skip + count]
        return 0

    lax.fori_loop(0, 2, attend, 0)

    for r in range(LEV * ROWS):
        nat_ref[r * PAD + COLS : (r + 1) * PAD, :] = jnp.zeros((PAD - COLS, D), F32)
    out_ref[...] = nat_ref[...].astype(BF16)


def attend_call(position, gain, tokens, north, south, west, east, pieces, interpret=False):
    vmem = pl.BlockSpec(memory_space=pltpu.VMEM)
    anywhere = pl.BlockSpec(memory_space=pl.ANY)
    return pl.pallas_call(
        functools.partial(attn_kernel, position, len(pieces)),
        out_shape=jax.ShapeDtypeStruct((FLAT, D), BF16),
        in_specs=[vmem] * 6 + [anywhere] * len(pieces),
        out_specs=vmem,
        scratch_shapes=[
            pltpu.VMEM((D, QKV), BF16),
            pltpu.VMEM((REG, 104, D), F32),
            pltpu.VMEM((LEV * REG, WINS, SLOT, D), BF16),
            pltpu.VMEM((LEV * ROWS, WINS, SLOT, D), BF16),
            pltpu.VMEM((LEV * REG, WINS, SLOT, 2 * D), BF16),
            pltpu.VMEM((FLAT, D), F32),
            pltpu.SemaphoreType.DMA,
        ],
        compiler_params=pltpu.CompilerParams(vmem_limit_bytes=VMEM),
        interpret=interpret,
        name="attention",
    )(gain, tokens, north, south, west, east, *pieces)


MLP_ROWS = 240


def mlp_kernel(position, n_w, gain_ref, tok_ref, att_ref, *refs):
    w_refs = refs[:n_w]
    out_ref, pu_ref, dn_ref, x_ref, sem = refs[n_w:]
    pos, _ = position()
    copies = []
    for mine, o, i, src in pieces_of(w_refs):
        shard = shard_row(pos, mine, o, i)
        at = pl.multiple_of(shard * 16, 16)
        copies.append(
            pltpu.make_async_copy(src.at[:, 0 : D + FF], pu_ref.at[pl.ds(at, 16), :], sem)
        )
        for n in range(4):
            at = pl.multiple_of(shard * 64 + 16 * n, 16)
            lo = D + FF + D * n
            copies.append(
                pltpu.make_async_copy(src.at[:, lo : lo + D], dn_ref.at[pl.ds(at, 16), :], sem)
            )
    for c in copies:
        c.start()
    for r in range(LEV * ROWS):
        x_ref[r * PAD : r * PAD + COLS, :] = tok_ref[r].astype(F32)
        x_ref[r * PAD + COLS : (r + 1) * PAD, :] = jnp.zeros((PAD - COLS, D), F32)
    for c in copies:
        c.wait()

    gain = gain_ref[...]

    def chunk(n, _):
        rows = pl.ds(pl.multiple_of(n * MLP_ROWS, 16), MLP_ROWS)
        residual = x_ref[rows, :] + jnp.dot(
            att_ref[rows, :], pu_ref[:, 0:D], preferred_element_type=F32
        )
        normed = norm(residual, gain).astype(BF16)
        total = residual
        for f in range(4):
            up = jnp.dot(
                normed, pu_ref[:, D + D * f : D + D * (f + 1)], preferred_element_type=F32
            )
            hidden = (0.5 * up * (1.0 + lax.erf(up * 0.7071067811865476))).astype(BF16)
            total = total + jnp.dot(
                hidden, dn_ref[D * f : D * (f + 1), :], preferred_element_type=F32
            )
        x_ref[rows, :] = total
        return 0

    lax.fori_loop(0, FLAT // MLP_ROWS, chunk, 0)
    for r in range(LEV * ROWS):
        out_ref[r] = x_ref[r * PAD : r * PAD + COLS, :].astype(BF16)


def mlp_call(position, gain, tokens, attended, pieces, interpret=False):
    vmem = pl.BlockSpec(memory_space=pltpu.VMEM)
    anywhere = pl.BlockSpec(memory_space=pl.ANY)
    return pl.pallas_call(
        functools.partial(mlp_kernel, position, len(pieces)),
        out_shape=jax.ShapeDtypeStruct((LEV * ROWS, COLS, D), BF16),
        in_specs=[vmem] * 3 + [anywhere] * len(pieces),
        out_specs=vmem,
        scratch_shapes=[
            pltpu.VMEM((D, D + FF), BF16),
            pltpu.VMEM((FF, D), BF16),
            pltpu.VMEM((FLAT, D), F32),
            pltpu.SemaphoreType.DMA,
        ],
        compiler_params=pltpu.CompilerParams(vmem_limit_bytes=VMEM),
        interpret=interpret,
        name="mlp",
    )(gain, tokens, attended, *pieces)


AXES = ("yh", "z", "x", "yl", "core")
SIZES = (2, 8, 4, 4, 2)


def number(yh, z, x, yl, core):
    return (((yh * 8 + z) * 4 + x) * 4 + yl) * 2 + core


def each_device():
    for yh in range(2):
        for z in range(8):
            for x in range(4):
                for yl in range(4):
                    for core in range(2):
                        yield yh, z, x, yl, core


def ring_pairs(by, first):
    pairs = []
    for yh, z, x, yl, core in each_device():
        if (core == 0) == first:
            y = (yh * 4 + yl + by) % 8
            to = number(y // 4, z, x, y % 4, core)
        else:
            to = number(yh, z, (x + by) % 4, yl, core)
        pairs.append((number(yh, z, x, yl, core), to))
    return pairs


def lat_pairs(by):
    pairs = []
    for yh, z, x, yl, core in each_device():
        band = yh * 8 + z + by
        if 0 <= band < 16:
            pairs.append((number(yh, z, x, yl, core), number(band // 8, band % 8, x, yl, core)))
    return pairs


def lon_pairs(by):
    pairs = []
    for yh, z, x, yl, core in each_device():
        lon = ((x * 4 + yl) * 2 + core + by) % 32
        pairs.append((number(yh, z, x, yl, core), number(yh, z, lon // 8, lon // 2 % 4, lon % 2)))
    return pairs


def core_pairs():
    return [(number(*d), number(*d[:4], 1 - d[4])) for d in each_device()]


def send(value, pairs):
    return lax.ppermute(value, AXES, pairs)


def gather_stage(block, first):
    return [
        block,
        send(block, ring_pairs(1, first)),
        send(block, ring_pairs(-1, first)),
        send(block, ring_pairs(2, first)),
    ]


def position():
    pos = (lax.axis_index("x"), lax.axis_index("yl"), lax.axis_index("core"))
    return pos, lax.axis_index("yh") * 8 + lax.axis_index("z")


def body(tokens, gain_attn, gain_mlp, w_qkv, w_proj, w_up, w_down):
    north = send(tokens[:, ROWS - HALF :], lat_pairs(1))
    south = send(tokens[:, :HALF], lat_pairs(-1))
    shard = jnp.concatenate(
        [w_qkv, w_proj, w_up] + [w_down[16 * n : 16 * n + 16] for n in range(4)], axis=1
    )
    line = jnp.stack(gather_stage(shard, True))
    region = jnp.concatenate([north, tokens, south], axis=1)
    west = send(region[:, :, COLS - RIM :], lon_pairs(1))
    east = send(region[:, :, :RIM], lon_pairs(-1))

    own_a = gather_stage(line[:, :, :QKV], False)
    other_a = send(jnp.concatenate(own_a, axis=0), core_pairs())
    own_b = gather_stage(line[:, :, QKV:], False)
    other_b = [
        send(jnp.concatenate(own_b[:2], axis=0), core_pairs()),
        send(jnp.concatenate(own_b[2:], axis=0), core_pairs()),
    ]
    attended = attend_call(
        position, gain_attn.reshape(1, D), tokens, north, south, west, east, own_a + [other_a]
    )
    done = mlp_call(
        position,
        gain_mlp.reshape(1, D),
        tokens.reshape(LEV * ROWS, COLS, D),
        attended,
        own_b + other_b,
    )
    return done.reshape(LEV, ROWS, COLS, D)


def solution(mesh):
    torus = Mesh(mesh.devices.reshape(SIZES), AXES)
    weight = P(("x", "yl", "core"), None)
    grid = P(None, ("yh", "z"), ("x", "yl", "core"), None)
    return jax.shard_map(
        body,
        mesh=torus,
        in_specs=(grid, P(), P(), weight, weight, weight, weight),
        out_specs=grid,
        check_vma=False,
    )
```

time: 285 us -> 139 us (0.49)
  waiting for transfers between devices: 131 us -> 34.1 us
  blocking collectives: 50.5 us -> 0 us
  starting transfers between devices: 18.6 us -> 62 us
  matrix products: 30 us -> 0 us
  Pallas kernels: 0 us -> 28.9 us
  local copies, waits for them, and re-layouts: 33.7 us -> 12.1 us
  between operations: 13.4 us -> 0.44 us
  other arithmetic: 7.14 us -> 0.36 us
    all_gather x3 -> x0, waiting for transfers between devices: 100 us -> none  [the longest x1 64 us: body(): lax.all_gather(w_down, 'lon', axis=0, tiled=True)]
    all_gather x1 -> x0, blocking collectives: 50.5 us -> none  [body(): lax.all_gather(w_proj, 'lon', axis=0, tiled=True)]
    ppermute x4 -> x16, starting transfers between devices: 18.5 us -> 62 us  [send(): return lax.ppermute(value, AXES, pairs)]
    dot_general x5 -> x0, matrix products: 30 us -> none  [the longest x1 19.4 us: down_apply(): return jnp.dot(hidden, full_down, preferred_element_type=jnp.float32)]
    pallas_call x0 -> x2, Pallas kernels: none -> 28.9 us  [the longest x1 15.5 us: attend_call(): pl.pallas_call(functools.partial(attn_kernel, position, len(pieces)), out...]
    reshape x4 -> x1, local copies, waits for them, and re-layouts: 12.7 us -> 2.8 us  [body(): return done.reshape(LEV, ROWS, COLS, D)]
    slice x5 -> x2, local copies, waits for them, and re-layouts: 5.15 us -> 0.2 us  [the longest x1 0.13 us: body(): east = send(region[:, :, :RIM], lon_pairs(-1))]
    convert_element_type x3 -> x0, local copies, waits for them, and re-layouts: 4.91 us -> none  [the longest x1 2.95 us: attend(): attended = jnp.einsum('whqk,whkd->whqd', probability, values, preferred_e...]
  transfers between devices with their start and end apart: 7 -> 16, of which waited for: 5 -> 7; matrix products, arithmetic and copies ran while one was open for 17% -> 1% of each run, Pallas kernels for 0% -> 11%
where the time goes in v1:
time: 139 us; the launch traced here: 138 us
  starting transfers between devices  62 us (45%)
  waiting for transfers between devices  34.1 us (25%)
  Pallas kernels  28.9 us (21%)
  local copies, waits for them, and re-layouts  12.1 us (9%)
    ppermute x16, starting transfers between devices, send(): return lax.ppermute(value, AXES, pairs)  62 us
    ppermute x16, waiting for transfers between devices, send(): return lax.ppermute(value, AXES, pairs)  34.1 us
    pallas_call x1, Pallas kernels, attend_call(): pl.pallas_call(functools.partial(attn_kernel, position, len(pieces)), out...  15.5 us
    pallas_call x1, Pallas kernels, mlp_call(): pl.pallas_call(functools.partial(mlp_kernel, position, len(pieces)), out_...  13.4 us
    unnamed x41, local copies, waits for them, and re-layouts  8.3 us
    reshape x1, local copies, waits for them, and re-layouts, body(): return done.reshape(LEV, ROWS, COLS, D)  2.8 us
  transfers between devices with their start and end apart: 16, of which 7 were waited for; matrix products, arithmetic and copies ran while one was open for 1% of the time, Pallas kernels for 11%

profile of v1, /device:TPU:1, one launch (start us, length us, event | category | flops | bytes accessed | tf_op | source)
XLA Modules:
  0.0 137.9 jit_solution(8934917022282388603)
XLA Ops:
  0.0 0.9 constant_dynamic-update-slice_fusion.9
  0.9 0.7 constant_dynamic-update-slice_fusion.8
  1.6 0.8 constant_dynamic-update-slice_fusion.7
  2.4 0.7 constant_dynamic-update-slice_fusion.6
  5.3 5.5 %collective-permute-start.6 = (bf16[16,6144]{1,0:T(8,128)(2,1)S(1)}, bf16[16,6144]{1,0:T(8,128)(2,1)S(1)}, u32[]{:S(2)}, u32[]{:S(2)}) collective-permute-start(bf16[16,6144]{1,0:T(8,128)(2,1)S(1)} %constant_dynamic-update-slice_fusion.3), channel_id=1, source_target_pairs={{0,4},{1,17},{2,6},{3,19},{4,256},{5,21},{6,258},{7,23},{8,12},{9,... | collective-permute-start | bytes 589832 | tf_op jit(solution)/shard_map/ppermute | solution.py:320
  10.8 2.8 %collective-permute-start.5 = (bf16[16,6144]{1,0:T(8,128)(2,1)S(1)}, bf16[16,6144]{1,0:T(8,128)(2,1)S(1)}, u32[]{:S(2)}, u32[]{:S(2)}) collective-permute-start(bf16[16,6144]{1,0:T(8,128)(2,1)S(1)} %constant_dynamic-update-slice_fusion.3), channel_id=1, source_target_pairs={{0,262},{1,25},{2,0},{3,27},{4,2},{5,29},{6,4},{7,31},{8,270},{9,1... | collective-permute-start | bytes 589832 | tf_op jit(solution)/shard_map/ppermute | solution.py:320
  13.6 2.5 %collective-permute-start.4 = (bf16[16,6144]{1,0:T(8,128)(2,1)S(1)}, bf16[16,6144]{1,0:T(8,128)(2,1)S(1)}, u32[]{:S(2)}, u32[]{:S(2)}) collective-permute-start(bf16[16,6144]{1,0:T(8,128)(2,1)S(1)} %constant_dynamic-update-slice_fusion.3), channel_id=1, source_target_pairs={{0,2},{1,9},{2,4},{3,11},{4,6},{5,13},{6,256},{7,15},{8,10},{9,17}... | collective-permute-start | bytes 589832 | tf_op jit(solution)/shard_map/ppermute | solution.py:320
  16.1 1.1 collective-permute-done.5
  17.2 4.3 %collective-permute-done.4 = bf16[16,6144]{1,0:T(8,128)(2,1)S(1)} collective-permute-done((bf16[16,6144]{1,0:T(8,128)(2,1)S(1)}, bf16[16,6144]{1,0:T(8,128)(2,1)S(1)}, u32[]{:S(2)}, u32[]{:S(2)}) %collective-permute-start.4) | collective-permute-done | bytes 196640 | tf_op jit(solution)/shard_map/ppermute | solution.py:320
  21.6 2.9 %collective-permute-start.11 = (bf16[4,16,4608]{2,1,0:T(8,128)(2,1)S(1)}, bf16[4,16,4608]{2,1,0:T(8,128)(2,1)S(1)}, u32[]{:S(2)}, u32[]{:S(2)}) collective-permute-start(bf16[4,16,4608]{2,1,0:T(8,128)(2,1)S(1)} %pad_maximum_fusion.3.refs_0_), channel_id=1, source_target_pairs={{0,8},{1,3},{2,10},{3,5},{4,12},{5,7},{6,14},{7,257},{8,16},{9,11}... | collective-permute-start | bytes 1769480 | tf_op jit(solution)/shard_map/ppermute | solution.py:320
  24.8 4.0 %collective-permute-start = (bf16[4,3,36,512]{3,2,1,0:T(8,128)(2,1)S(1)}, bf16[4,3,36,512]{3,2,1,0:T(8,128)(2,1)S(1)}, u32[]{:S(2)}, u32[]{:S(2)}) collective-permute-start(bf16[4,3,36,512]{3,2,1,0:T(8,128)(2,1)S(1)} %get-tuple-element.8), channel_id=1, source_target_pairs={{0,32},{1,33},{2,34},{3,35},{4,36},{5,37},{6,38},{7,39},{8,40},{9,... | collective-permute-start | bytes 1327112 | tf_op jit(solution)/shard_map/ppermute | solution.py:320
  28.8 1.3 collective-permute-start.1
  30.1 16.1 %collective-permute-start.12 = (bf16[4,16,4608]{2,1,0:T(8,128)(2,1)S(1)}, bf16[4,16,4608]{2,1,0:T(8,128)(2,1)S(1)}, u32[]{:S(2)}, u32[]{:S(2)}) collective-permute-start(bf16[4,16,4608]{2,1,0:T(8,128)(2,1)S(1)} %pad_maximum_fusion.3.refs_0_), channel_id=1, source_target_pairs={{0,24},{1,263},{2,26},{3,1},{4,28},{5,3},{6,30},{7,5},{8,0},{9,271... | collective-permute-start | bytes 1769480 | tf_op jit(solution)/shard_map/ppermute | solution.py:320
  46.2 1.9 %collective-permute-start.13 = (bf16[4,16,4608]{2,1,0:T(8,128)(2,1)S(1)}, bf16[4,16,4608]{2,1,0:T(8,128)(2,1)S(1)}, u32[]{:S(2)}, u32[]{:S(2)}) collective-permute-start(bf16[4,16,4608]{2,1,0:T(8,128)(2,1)S(1)} %pad_maximum_fusion.3.refs_0_), channel_id=1, source_target_pairs={{0,16},{1,5},{2,18},{3,7},{4,20},{5,257},{6,22},{7,259},{8,24},{9,... | collective-permute-start | bytes 1769480 | tf_op jit(solution)/shard_map/ppermute | solution.py:320
  48.2 1.9 %collective-permute-start.7 = (bf16[4,16,1536]{2,1,0:T(8,128)(2,1)S(1)}, bf16[4,16,1536]{2,1,0:T(8,128)(2,1)S(1)}, u32[]{:S(2)}, u32[]{:S(2)}) collective-permute-start(bf16[4,16,1536]{2,1,0:T(8,128)(2,1)S(1)} %pad_maximum_fusion.6.refs_0_), channel_id=1, source_target_pairs={{0,8},{1,3},{2,10},{3,5},{4,12},{5,7},{6,14},{7,257},{8,16},{9,11}... | collective-permute-start | bytes 589832 | tf_op jit(solution)/shard_map/ppermute | solution.py:320
  50.3 2.8 %collective-permute-done.12.refs_2_ = bf16[4,16,4608]{2,1,0:T(8,128)(2,1)S(1)} collective-permute-done((bf16[4,16,4608]{2,1,0:T(8,128)(2,1)S(1)}, bf16[4,16,4608]{2,1,0:T(8,128)(2,1)S(1)}, u32[]{:S(2)}, u32[]{:S(2)}) %collective-permute-start.12) | collective-permute-done | bytes 589856 | tf_op jit(solution)/shard_map/ppermute | solution.py:320
  53.0 10.6 %collective-permute-start.8 = (bf16[4,16,1536]{2,1,0:T(8,128)(2,1)S(1)}, bf16[4,16,1536]{2,1,0:T(8,128)(2,1)S(1)}, u32[]{:S(2)}, u32[]{:S(2)}) collective-permute-start(bf16[4,16,1536]{2,1,0:T(8,128)(2,1)S(1)} %pad_maximum_fusion.6.refs_0_), channel_id=1, source_target_pairs={{0,24},{1,263},{2,26},{3,1},{4,28},{5,3},{6,30},{7,5},{8,0},{9,271... | collective-permute-start | bytes 589832 | tf_op jit(solution)/shard_map/ppermute | solution.py:320
  63.6 13.6 %collective-permute-done.13.refs_3_ = bf16[4,16,4608]{2,1,0:T(8,128)(2,1)S(1)} collective-permute-done((bf16[4,16,4608]{2,1,0:T(8,128)(2,1)S(1)}, bf16[4,16,4608]{2,1,0:T(8,128)(2,1)S(1)}, u32[]{:S(2)}, u32[]{:S(2)}) %collective-permute-start.13) | collective-permute-done | bytes 589856 | tf_op jit(solution)/shard_map/ppermute | solution.py:320
  77.2 1.9 %collective-permute-start.9 = (bf16[4,16,1536]{2,1,0:T(8,128)(2,1)S(1)}, bf16[4,16,1536]{2,1,0:T(8,128)(2,1)S(1)}, u32[]{:S(2)}, u32[]{:S(2)}) collective-permute-start(bf16[4,16,1536]{2,1,0:T(8,128)(2,1)S(1)} %pad_maximum_fusion.6.refs_0_), channel_id=1, source_target_pairs={{0,16},{1,5},{2,18},{3,7},{4,20},{5,257},{6,22},{7,259},{8,24},{9,... | collective-permute-start | bytes 589832 | tf_op jit(solution)/shard_map/ppermute | solution.py:320
  79.2 1.9 %collective-permute-start.14 = (bf16[8,16,4608]{2,1,0:T(8,128)(2,1)S(1)}, bf16[8,16,4608]{2,1,0:T(8,128)(2,1)S(1)}, u32[]{:S(2)}, u32[]{:S(2)}) collective-permute-start(bf16[8,16,4608]{2,1,0:T(8,128)(2,1)S(1)} %pad_maximum_fusion), channel_id=1, source_target_pairs={{0,1},{1,0},{2,3},{3,2},{4,5},{5,4},{6,7},{7,6},{8,9},{9,8},{10,11... | collective-permute-start | bytes 3538952 | tf_op jit(solution)/shard_map/ppermute | solution.py:320
  81.2 2.4 %collective-permute-start.15 = (bf16[8,16,4608]{2,1,0:T(8,128)(2,1)S(1)}, bf16[8,16,4608]{2,1,0:T(8,128)(2,1)S(1)}, u32[]{:S(2)}, u32[]{:S(2)}) collective-permute-start(bf16[8,16,4608]{2,1,0:T(8,128)(2,1)S(1)} %pad_maximum_fusion.1), channel_id=1, source_target_pairs={{0,1},{1,0},{2,3},{3,2},{4,5},{5,4},{6,7},{7,6},{8,9},{9,8},{10,11... | collective-permute-start | bytes 3538952 | tf_op jit(solution)/shard_map/ppermute | solution.py:320
  83.6 2.1 %collective-permute-done.9.refs_3_ = bf16[4,16,1536]{2,1,0:T(8,128)(2,1)S(1)} collective-permute-done((bf16[4,16,1536]{2,1,0:T(8,128)(2,1)S(1)}, bf16[4,16,1536]{2,1,0:T(8,128)(2,1)S(1)}, u32[]{:S(2)}, u32[]{:S(2)}) %collective-permute-start.9) | collective-permute-done | bytes 196640 | tf_op jit(solution)/shard_map/ppermute | solution.py:320
  85.8 1.9 %collective-permute-start.10 = (bf16[16,16,1536]{2,1,0:T(8,128)(2,1)S(1)}, bf16[16,16,1536]{2,1,0:T(8,128)(2,1)}, u32[]{:S(2)}, u32[]{:S(2)}) collective-permute-start(bf16[16,16,1536]{2,1,0:T(8,128)(2,1)S(1)} %pad_maximum_fusion.2), channel_id=1, source_target_pairs={{0,1},{1,0},{2,3},{3,2},{4,5},{5,4},{6,7},{7,6},{8,9},{9,8},{10,11... | collective-permute-start | bytes 2359304 | tf_op jit(solution)/shard_map/ppermute | solution.py:320
  89.4 1.9 %collective-permute-start.2 = (bf16[4,12,6,512]{3,2,1,0:T(8,128)(2,1)S(1)}, bf16[4,12,6,512]{3,2,1,0:T(8,128)(2,1)S(1)}, u32[]{:S(2)}, u32[]{:S(2)}) collective-permute-start(bf16[4,12,6,512]{3,2,1,0:T(8,128)(2,1)S(1)} %get-tuple-element.6), channel_id=1, source_target_pairs={{0,1},{1,2},{2,3},{3,4},{4,5},{5,6},{6,7},{7,8},{8,9},{9,10},{10,1... | collective-permute-start | bytes 884744 | tf_op jit(solution)/shard_map/ppermute | solution.py:320
  91.3 2.4 %collective-permute-start.3 = (bf16[4,12,6,512]{3,2,1,0:T(8,128)(2,1)S(1)}, bf16[4,12,6,512]{3,2,1,0:T(8,128)(2,1)S(1)}, u32[]{:S(2)}, u32[]{:S(2)}) collective-permute-start(bf16[4,12,6,512]{3,2,1,0:T(8,128)(2,1)S(1)} %get-tuple-element.5), channel_id=1, source_target_pairs={{0,31},{1,0},{2,1},{3,2},{4,3},{5,4},{6,5},{7,6},{8,7},{9,8},{10,9... | collective-permute-start | bytes 884744 | tf_op jit(solution)/shard_map/ppermute | solution.py:320
  93.7 2.3 %collective-permute-done.2.west_ref = bf16[4,12,6,512]{3,2,1,0:T(8,128)(2,1)S(1)} collective-permute-done((bf16[4,12,6,512]{3,2,1,0:T(8,128)(2,1)S(1)}, bf16[4,12,6,512]{3,2,1,0:T(8,128)(2,1)S(1)}, u32[]{:S(2)}, u32[]{:S(2)}) %collective-permute-start.2) | collective-permute-done | bytes 294944 | tf_op jit(solution)/shard_map/ppermute | solution.py:320
  96.0 8.0 %collective-permute-done.3.east_ref = bf16[4,12,6,512]{3,2,1,0:T(8,128)(2,1)S(1)} collective-permute-done((bf16[4,12,6,512]{3,2,1,0:T(8,128)(2,1)S(1)}, bf16[4,12,6,512]{3,2,1,0:T(8,128)(2,1)S(1)}, u32[]{:S(2)}, u32[]{:S(2)}) %collective-permute-start.3) | collective-permute-done | bytes 294944 | tf_op jit(solution)/shard_map/ppermute | solution.py:320
  104.0 0.7 copy-done.15
  104.7 15.5 %attention.1.att_ref = bf16[960,512]{1,0:T(8,128)(2,1)} custom-call(f32[1,512]{1,0:T(1,128)} %bitcast.18, bf16[4,6,36,512]{3,2,1,0:T(8,128)(2,1)} %copy-done, bf16[4,3,36,512]{3,2,1,0:T(8,128)(2,1)} %copy-done.6, bf16[4,3,36,512]{3,2,1,0:T(8,128)(2,1)} %copy-done.7, bf16[4,12,6,512]{3,2,1,0:T(8,128)(2,1)} %copy-done.14, bf16[4,12,6,512]{3,2,1,0:T(8,128)(2,1)} %copy-done.15, ...), custom_call_target="tpu_custom_call" | custom-call | tf_op jit(solution)/shard_map/attention/pallas_call | solution.py:176
  120.3 1.0 copy-done.9
  121.7 13.4 %mlp.1 = bf16[24,36,512]{2,1,0:T(8,128)(2,1)} custom-call(f32[1,512]{1,0:T(1,128)} %bitcast.19, bf16[24,36,512]{2,1,0:T(8,128)(2,1)} %bitcast.8, bf16[960,512]{1,0:T(8,128)(2,1)} %attention.1.att_ref, bf16[4,16,4608]{2,1,0:T(8,128)(2,1)} %copy-done.1, bf16[4,16,4608]{2,1,0:T(8,128)(2,1)} %copy-done.3, bf16[4,16,4608]{2,1,0:T(8,128)(2,1)} %copy-done.4, ...), custom_call_target="tpu_custom_call" | custom-call | tf_op jit(solution)/shard_map/mlp/pallas_call | solution.py:252
  135.1 2.8 %copy.13 = bf16[4,6,36,512]{3,0,2,1:T(4,128)(2,1)} copy(bf16[4,6,36,512]{3,2,1,0:T(8,128)(2,1)} %bitcast.9) | data formatting | bytes 1769472 | tf_op jit(solution)/shard_map/reshape | solution.py:365
  (53 shorter events, 4.8 us)
Async XLA Ops:
  0.0 24.5 %copy-start.2 = (bf16[4,6,36,512]{3,0,2,1:T(4,128)(2,1)S(1)}, bf16[4,6,36,512]{3,0,2,1:T(4,128)(2,1)}, u32[]{:S(2)}) copy-start(bf16[4,6,36,512]{3,0,2,1:T(4,128)(2,1)} %param.7) | copy-start | bytes 2654212
  5.3 10.8 %collective-permute-start.6 = (bf16[16,6144]{1,0:T(8,128)(2,1)S(1)}, bf16[16,6144]{1,0:T(8,128)(2,1)S(1)}, u32[]{:S(2)}, u32[]{:S(2)}) collective-permute-start(bf16[16,6144]{1,0:T(8,128)(2,1)S(1)} %constant_dynamic-update-slice_fusion.3), channel_id=1, source_target_pairs={{0,4},{1,17},{2,6},{3,19},{4,256},{5,21},{6,258},{7,23},{8,12},{9,... | collective-permute-start | bytes 589832 | tf_op jit(solution)/shard_map/ppermute | solution.py:320
  10.8 6.4 %collective-permute-start.5 = (bf16[16,6144]{1,0:T(8,128)(2,1)S(1)}, bf16[16,6144]{1,0:T(8,128)(2,1)S(1)}, u32[]{:S(2)}, u32[]{:S(2)}) collective-permute-start(bf16[16,6144]{1,0:T(8,128)(2,1)S(1)} %constant_dynamic-update-slice_fusion.3), channel_id=1, source_target_pairs={{0,262},{1,25},{2,0},{3,27},{4,2},{5,29},{6,4},{7,31},{8,270},{9,1... | collective-permute-start | bytes 589832 | tf_op jit(solution)/shard_map/ppermute | solution.py:320
  13.6 7.9 %collective-permute-start.4 = (bf16[16,6144]{1,0:T(8,128)(2,1)S(1)}, bf16[16,6144]{1,0:T(8,128)(2,1)S(1)}, u32[]{:S(2)}, u32[]{:S(2)}) collective-permute-start(bf16[16,6144]{1,0:T(8,128)(2,1)S(1)} %constant_dynamic-update-slice_fusion.3), channel_id=1, source_target_pairs={{0,2},{1,9},{2,4},{3,11},{4,6},{5,13},{6,256},{7,15},{8,10},{9,17}... | collective-permute-start | bytes 589832 | tf_op jit(solution)/shard_map/ppermute | solution.py:320
  21.5 28.6 %copy-start.1 = (bf16[4,16,4608]{2,1,0:T(8,128)(2,1)}, bf16[4,16,4608]{2,1,0:T(8,128)(2,1)S(1)}, u32[]{:S(2)}) copy-start(bf16[4,16,4608]{2,1,0:T(8,128)(2,1)S(1)} %pad_maximum_fusion.3.refs_0_) | copy-start | bytes 1769476
  21.6 26.6 %collective-permute-start.11 = (bf16[4,16,4608]{2,1,0:T(8,128)(2,1)S(1)}, bf16[4,16,4608]{2,1,0:T(8,128)(2,1)S(1)}, u32[]{:S(2)}, u32[]{:S(2)}) collective-permute-start(bf16[4,16,4608]{2,1,0:T(8,128)(2,1)S(1)} %pad_maximum_fusion.3.refs_0_), channel_id=1, source_target_pairs={{0,8},{1,3},{2,10},{3,5},{4,12},{5,7},{6,14},{7,257},{8,16},{9,11}... | collective-permute-start | bytes 1769480 | tf_op jit(solution)/shard_map/ppermute | solution.py:320
  24.7 23.5 %copy-start = (bf16[4,6,36,512]{3,2,1,0:T(8,128)(2,1)}, bf16[4,6,36,512]{3,2,1,0:T(8,128)(2,1)S(1)}, u32[]{:S(2)}) copy-start(bf16[4,6,36,512]{3,2,1,0:T(8,128)(2,1)S(1)} %copy.8.tok_ref) | copy-start | bytes 2654212
  24.8 63.0 %collective-permute-start = (bf16[4,3,36,512]{3,2,1,0:T(8,128)(2,1)S(1)}, bf16[4,3,36,512]{3,2,1,0:T(8,128)(2,1)S(1)}, u32[]{:S(2)}, u32[]{:S(2)}) collective-permute-start(bf16[4,3,36,512]{3,2,1,0:T(8,128)(2,1)S(1)} %get-tuple-element.8), channel_id=1, source_target_pairs={{0,32},{1,33},{2,34},{3,35},{4,36},{5,37},{6,38},{7,39},{8,40},{9,... | collective-permute-start | bytes 1327112 | tf_op jit(solution)/shard_map/ppermute | solution.py:320
  28.8 59.8 %collective-permute-start.1 = (bf16[4,3,36,512]{3,2,1,0:T(8,128)(2,1)S(1)}, bf16[4,3,36,512]{3,2,1,0:T(8,128)(2,1)S(1)}, u32[]{:S(2)}, u32[]{:S(2)}) collective-permute-start(bf16[4,3,36,512]{3,2,1,0:T(8,128)(2,1)S(1)} %get-tuple-element.7), channel_id=1, source_target_pairs={{32,0},{33,1},{34,2},{35,3},{36,4},{37,5},{38,6},{39,7},{40,8},{41... | collective-permute-start | bytes 1327112 | tf_op jit(solution)/shard_map/ppermute | solution.py:320
  30.1 22.9 %collective-permute-start.12 = (bf16[4,16,4608]{2,1,0:T(8,128)(2,1)S(1)}, bf16[4,16,4608]{2,1,0:T(8,128)(2,1)S(1)}, u32[]{:S(2)}, u32[]{:S(2)}) collective-permute-start(bf16[4,16,4608]{2,1,0:T(8,128)(2,1)S(1)} %pad_maximum_fusion.3.refs_0_), channel_id=1, source_target_pairs={{0,24},{1,263},{2,26},{3,1},{4,28},{5,3},{6,30},{7,5},{8,0},{9,271... | collective-permute-start | bytes 1769480 | tf_op jit(solution)/shard_map/ppermute | solution.py:320
  46.2 31.0 %collective-permute-start.13 = (bf16[4,16,4608]{2,1,0:T(8,128)(2,1)S(1)}, bf16[4,16,4608]{2,1,0:T(8,128)(2,1)S(1)}, u32[]{:S(2)}, u32[]{:S(2)}) collective-permute-start(bf16[4,16,4608]{2,1,0:T(8,128)(2,1)S(1)} %pad_maximum_fusion.3.refs_0_), channel_id=1, source_target_pairs={{0,16},{1,5},{2,18},{3,7},{4,20},{5,257},{6,22},{7,259},{8,24},{9,... | collective-permute-start | bytes 1769480 | tf_op jit(solution)/shard_map/ppermute | solution.py:320
  48.2 37.5 %copy-start.8 = (bf16[4,16,1536]{2,1,0:T(8,128)(2,1)}, bf16[4,16,1536]{2,1,0:T(8,128)(2,1)S(1)}, u32[]{:S(2)}) copy-start(bf16[4,16,1536]{2,1,0:T(8,128)(2,1)S(1)} %pad_maximum_fusion.6.refs_0_) | copy-start | bytes 589828
  48.2 2.1 %copy-start.3 = (bf16[4,16,4608]{2,1,0:T(8,128)(2,1)}, bf16[4,16,4608]{2,1,0:T(8,128)(2,1)S(1)}, u32[]{:S(2)}) copy-start(bf16[4,16,4608]{2,1,0:T(8,128)(2,1)S(1)} %collective-permute-done.11.refs_1_) | copy-start | bytes 1769476
  48.2 31.0 %collective-permute-start.7 = (bf16[4,16,1536]{2,1,0:T(8,128)(2,1)S(1)}, bf16[4,16,1536]{2,1,0:T(8,128)(2,1)S(1)}, u32[]{:S(2)}, u32[]{:S(2)}) collective-permute-start(bf16[4,16,1536]{2,1,0:T(8,128)(2,1)S(1)} %pad_maximum_fusion.6.refs_0_), channel_id=1, source_target_pairs={{0,8},{1,3},{2,10},{3,5},{4,12},{5,7},{6,14},{7,257},{8,16},{9,11}... | collective-permute-start | bytes 589832 | tf_op jit(solution)/shard_map/ppermute | solution.py:320
  53.0 32.8 %copy-start.4 = (bf16[4,16,4608]{2,1,0:T(8,128)(2,1)}, bf16[4,16,4608]{2,1,0:T(8,128)(2,1)S(1)}, u32[]{:S(2)}) copy-start(bf16[4,16,4608]{2,1,0:T(8,128)(2,1)S(1)} %collective-permute-done.12.refs_2_) | copy-start | bytes 1769476
  53.0 28.2 %collective-permute-start.8 = (bf16[4,16,1536]{2,1,0:T(8,128)(2,1)S(1)}, bf16[4,16,1536]{2,1,0:T(8,128)(2,1)S(1)}, u32[]{:S(2)}, u32[]{:S(2)}) collective-permute-start(bf16[4,16,1536]{2,1,0:T(8,128)(2,1)S(1)} %pad_maximum_fusion.6.refs_0_), channel_id=1, source_target_pairs={{0,24},{1,263},{2,26},{3,1},{4,28},{5,3},{6,30},{7,5},{8,0},{9,271... | collective-permute-start | bytes 589832 | tf_op jit(solution)/shard_map/ppermute | solution.py:320
  77.2 8.6 %copy-start.5 = (bf16[4,16,4608]{2,1,0:T(8,128)(2,1)}, bf16[4,16,4608]{2,1,0:T(8,128)(2,1)S(1)}, u32[]{:S(2)}) copy-start(bf16[4,16,4608]{2,1,0:T(8,128)(2,1)S(1)} %collective-permute-done.13.refs_3_) | copy-start | bytes 1769476
  77.2 8.5 %collective-permute-start.9 = (bf16[4,16,1536]{2,1,0:T(8,128)(2,1)S(1)}, bf16[4,16,1536]{2,1,0:T(8,128)(2,1)S(1)}, u32[]{:S(2)}, u32[]{:S(2)}) collective-permute-start(bf16[4,16,1536]{2,1,0:T(8,128)(2,1)S(1)} %pad_maximum_fusion.6.refs_0_), channel_id=1, source_target_pairs={{0,16},{1,5},{2,18},{3,7},{4,20},{5,257},{6,22},{7,259},{8,24},{9,... | collective-permute-start | bytes 589832 | tf_op jit(solution)/shard_map/ppermute | solution.py:320
  79.2 8.6 %copy-start.11 = (bf16[4,16,1536]{2,1,0:T(8,128)(2,1)}, bf16[4,16,1536]{2,1,0:T(8,128)(2,1)S(1)}, u32[]{:S(2)}) copy-start(bf16[4,16,1536]{2,1,0:T(8,128)(2,1)S(1)} %collective-permute-done.7.refs_1_) | copy-start | bytes 589828
  79.2 41.0 %collective-permute-start.14 = (bf16[8,16,4608]{2,1,0:T(8,128)(2,1)S(1)}, bf16[8,16,4608]{2,1,0:T(8,128)(2,1)S(1)}, u32[]{:S(2)}, u32[]{:S(2)}) collective-permute-start(bf16[8,16,4608]{2,1,0:T(8,128)(2,1)S(1)} %pad_maximum_fusion), channel_id=1, source_target_pairs={{0,1},{1,0},{2,3},{3,2},{4,5},{5,4},{6,7},{7,6},{8,9},{9,8},{10,11... | collective-permute-start | bytes 3538952 | tf_op jit(solution)/shard_map/ppermute | solution.py:320
  81.2 6.6 %copy-start.12 = (bf16[4,16,1536]{2,1,0:T(8,128)(2,1)}, bf16[4,16,1536]{2,1,0:T(8,128)(2,1)S(1)}, u32[]{:S(2)}) copy-start(bf16[4,16,1536]{2,1,0:T(8,128)(2,1)S(1)} %collective-permute-done.8.refs_2_) | copy-start | bytes 589828
  81.2 39.1 %collective-permute-start.15 = (bf16[8,16,4608]{2,1,0:T(8,128)(2,1)S(1)}, bf16[8,16,4608]{2,1,0:T(8,128)(2,1)S(1)}, u32[]{:S(2)}, u32[]{:S(2)}) collective-permute-start(bf16[8,16,4608]{2,1,0:T(8,128)(2,1)S(1)} %pad_maximum_fusion.1), channel_id=1, source_target_pairs={{0,1},{1,0},{2,3},{3,2},{4,5},{5,4},{6,7},{7,6},{8,9},{9,8},{10,11... | collective-permute-start | bytes 3538952 | tf_op jit(solution)/shard_map/ppermute | solution.py:320
  85.7 2.1 %copy-start.13 = (bf16[4,16,1536]{2,1,0:T(8,128)(2,1)}, bf16[4,16,1536]{2,1,0:T(8,128)(2,1)S(1)}, u32[]{:S(2)}) copy-start(bf16[4,16,1536]{2,1,0:T(8,128)(2,1)S(1)} %collective-permute-done.9.refs_3_) | copy-start | bytes 589828
  85.8 18.2 %collective-permute-start.10 = (bf16[16,16,1536]{2,1,0:T(8,128)(2,1)S(1)}, bf16[16,16,1536]{2,1,0:T(8,128)(2,1)}, u32[]{:S(2)}, u32[]{:S(2)}) collective-permute-start(bf16[16,16,1536]{2,1,0:T(8,128)(2,1)S(1)} %pad_maximum_fusion.2), channel_id=1, source_target_pairs={{0,1},{1,0},{2,3},{3,2},{4,5},{5,4},{6,7},{7,6},{8,9},{9,8},{10,11... | collective-permute-start | bytes 2359304 | tf_op jit(solution)/shard_map/ppermute | solution.py:320
  87.8 0.8 copy-start.6
  88.6 0.8 copy-start.7
  89.4 6.6 %collective-permute-start.2 = (bf16[4,12,6,512]{3,2,1,0:T(8,128)(2,1)S(1)}, bf16[4,12,6,512]{3,2,1,0:T(8,128)(2,1)S(1)}, u32[]{:S(2)}, u32[]{:S(2)}) collective-permute-start(bf16[4,12,6,512]{3,2,1,0:T(8,128)(2,1)S(1)} %get-tuple-element.6), channel_id=1, source_target_pairs={{0,1},{1,2},{2,3},{3,4},{4,5},{5,6},{6,7},{7,8},{8,9},{9,10},{10,1... | collective-permute-start | bytes 884744 | tf_op jit(solution)/shard_map/ppermute | solution.py:320
  91.3 12.7 %collective-permute-start.3 = (bf16[4,12,6,512]{3,2,1,0:T(8,128)(2,1)S(1)}, bf16[4,12,6,512]{3,2,1,0:T(8,128)(2,1)S(1)}, u32[]{:S(2)}, u32[]{:S(2)}) collective-permute-start(bf16[4,12,6,512]{3,2,1,0:T(8,128)(2,1)S(1)} %get-tuple-element.5), channel_id=1, source_target_pairs={{0,31},{1,0},{2,1},{3,2},{4,3},{5,4},{6,5},{7,6},{8,7},{9,8},{10,9... | collective-permute-start | bytes 884744 | tf_op jit(solution)/shard_map/ppermute | solution.py:320
  96.0 8.0 %copy-start.14 = (bf16[4,12,6,512]{3,2,1,0:T(8,128)(2,1)}, bf16[4,12,6,512]{3,2,1,0:T(8,128)(2,1)S(1)}, u32[]{:S(2)}) copy-start(bf16[4,12,6,512]{3,2,1,0:T(8,128)(2,1)S(1)} %collective-permute-done.2.west_ref) | copy-start | bytes 884740
  104.0 0.7 copy-start.15
  120.3 1.0 copy-start.9
  120.3 1.4 %copy-start.10 = (bf16[8,16,4608]{2,1,0:T(8,128)(2,1)}, bf16[8,16,4608]{2,1,0:T(8,128)(2,1)S(1)}, u32[]{:S(2)}) copy-start(bf16[8,16,4608]{2,1,0:T(8,128)(2,1)S(1)} %collective-permute-done.15.refs_5_) | copy-start | bytes 3538948

commit v2 on v1

v2 whole, which is shorter than its diff:
```python
import functools

import jax
import jax.numpy as jnp
from jax import lax
from jax.experimental import pallas as pl
from jax.experimental.pallas import tpu as pltpu
from jax.sharding import Mesh
from jax.sharding import PartitionSpec as P

BF16 = jnp.bfloat16
F32 = jnp.float32
LEV, ROWS, COLS, D = 4, 6, 36, 512
HALF, RIM = 3, 6
REG = ROWS + 2 * HALF
SLOT = 16
WINS = 4
LINE = COLS * LEV
EDGE = RIM * LEV
STRIP = 32
REGION = LINE + 2 * STRIP
DIRECT = 80
WIDE = LINE + 2 * EDGE
SPREAD = WINS * LEV * SLOT
FF = 2048
QKV = 3 * D
REST = D + FF + 4 * D
OFFSETS = (0, 3, 1, 2)
VMEM = 56 * 1024 * 1024


def norm(values, gain):
    center = values - jnp.mean(values, axis=-1, keepdims=True)
    spread = jnp.mean(center * center, axis=-1, keepdims=True)
    return center * lax.rsqrt(spread + 1e-05) * gain


def whole():
    return pl.BlockSpec(memory_space=pltpu.VMEM)


def anywhere():
    return pl.BlockSpec(memory_space=pltpu.HBM)


def pack_kernel(position, gain_ref, tok_ref, qkv_ref, proj_ref, up_ref, down_ref, *outs):
    w_ref, top_ref, low_ref, direct_ref, hop_ref = outs
    w_ref[:, 0:QKV] = qkv_ref[...]
    w_ref[:, QKV : QKV + D] = proj_ref[...]
    w_ref[:, QKV + D : QKV + D + FF] = up_ref[...]
    for n in range(4):
        lo = QKV + D + FF + D * n
        w_ref[:, lo : lo + D] = down_ref[16 * n : 16 * n + 16, :]
    gain = gain_ref[...]
    for r in range(HALF):
        for out_ref, n in ((top_ref, r), (low_ref, r + HALF)):
            line = tok_ref[n].astype(F32).reshape(LINE, D)
            out_ref[r] = norm(line, gain).astype(BF16)
    band = position()[1]

    def middle(ref):
        direct_ref[...] = ref[:, 0:DIRECT, :]
        hop_ref[...] = ref[:, DIRECT:LINE, :]

    @pl.when(band == 7)
    def _():
        middle(low_ref)

    @pl.when(band != 7)
    def _():
        middle(top_ref)


def pack_call(position, gain, tokens, w_qkv, w_proj, w_up, w_down):
    def rows(n):
        return jax.ShapeDtypeStruct((HALF, n, D), BF16)

    return pl.pallas_call(
        functools.partial(pack_kernel, position),
        out_shape=[
            jax.ShapeDtypeStruct((16, QKV + REST), BF16),
            rows(LINE),
            rows(LINE),
            rows(DIRECT),
            rows(LINE - DIRECT),
        ],
        in_specs=[whole()] * 6,
        out_specs=[whole()] * 5,
        compiler_params=pltpu.CompilerParams(vmem_limit_bytes=VMEM),
        name="pack",
    )(gain, tokens, w_qkv, w_proj, w_up, w_down)


def place(pos, mine, other, moves):
    x, y, core = pos
    spans = ((0, 0, 4), (3, 0, 4), (1, 0, 4), (2, 0, 2), (2, 2, 2))

    def copies(own_is_first, move):
        low, count, target, sem = move
        result = []
        for refs, first in ((mine, own_is_first), (other, not own_is_first)):
            for source, (offset, start, size) in zip(refs, spans):
                inner = slice(start, start + size)
                if first:
                    where = (lax.rem(x + offset, 4), inner, 0)
                else:
                    where = (inner, lax.rem(y + offset, 4), 1)
                result.append(
                    pltpu.make_async_copy(source.at[:, :, low : low + count], target(where), sem)
                )
        return result

    def each(move, act):
        for own_is_first in (True, False):

            @pl.when(core == (0 if own_is_first else 1))
            def _(own_is_first=own_is_first):
                for c in copies(own_is_first, move):
                    act(c)

    for move in moves:
        each(move, lambda c: c.start())
    return [lambda move=move: each(move, lambda c: c.wait()) for move in moves]


def edge_kernel(position, top_ref, low_ref, north_ref, south_ref, direct_ref, hop_ref, east_ref, west_ref):
    band = position()[1]
    ends = ((east_ref, slice(LINE - STRIP, LINE), hop_ref, slice(LINE - DIRECT - STRIP, LINE - DIRECT)),
            (west_ref, slice(0, STRIP), direct_ref, slice(0, STRIP)))
    for out_ref, cols, middle_ref, middle_cols in ends:
        out_ref[0:HALF] = north_ref[:, cols, :]
        out_ref[HALF : 2 * HALF] = top_ref[:, cols, :]
        out_ref[2 * HALF : 3 * HALF] = low_ref[:, cols, :]
        out_ref[3 * HALF :] = south_ref[:, cols, :]

        @pl.when(band == 8)
        def _():
            out_ref[0:HALF] = middle_ref[:, middle_cols, :]

        @pl.when(band == 7)
        def _():
            out_ref[3 * HALF :] = middle_ref[:, middle_cols, :]


def edge_call(position, *halo):
    return pl.pallas_call(
        functools.partial(edge_kernel, position),
        out_shape=[jax.ShapeDtypeStruct((REG, STRIP, D), BF16)] * 2,
        in_specs=[whole()] * 6,
        out_specs=[whole()] * 2,
        compiler_params=pltpu.CompilerParams(vmem_limit_bytes=VMEM),
        cost_estimate=pl.CostEstimate(
            flops=10**10, transcendentals=0, bytes_accessed=8 * 1024 * 1024
        ),
        name="edges",
    )(*halo)


def slot_source(index):
    j = index // (LEV * SLOT)
    level = lax.rem(index // SLOT, LEV)
    col = lax.rem(index, SLOT)
    return jnp.where(col < 2 * RIM, (j * 2 * RIM + col) * LEV + level, -1)


CHUNK_ROWS = 3


def block_kernel(position, gain_ref, tok_hbm, *refs):
    top, low, north, south, direct, hop, west, east = refs[:8]
    mine, (near, rest), out_ref = refs[8:13], refs[13:15], refs[15]
    other = [near.at[0:4], near.at[4:8], near.at[8:12], rest.at[0:2], rest.at[2:4]]
    tok_ref, reg_ref, w_ref, pu_ref, dn_ref, q_ref, kv_ref, att_ref = refs[16:24]
    tok_sem, reg_sem, w_sem, pu_sem, dn_sem = refs[24:]
    pos, band = position()
    fetch = pltpu.make_async_copy(tok_hbm, tok_ref, tok_sem)
    main = slice(STRIP, STRIP + LINE)
    first = slice(STRIP, STRIP + DIRECT)
    second = slice(STRIP + DIRECT, STRIP + LINE)

    def into(source, rows, cols):
        return pltpu.make_async_copy(source, reg_ref.at[rows, cols], reg_sem)

    above, below = slice(0, HALF), slice(3 * HALF, REG)
    always = [
        into(top, slice(HALF, 2 * HALF), main),
        into(low, slice(2 * HALF, 3 * HALF), main),
        into(west, slice(0, REG), slice(0, STRIP)),
        into(east, slice(0, REG), slice(STRIP + LINE, REGION)),
    ]
    from_north, from_south = into(north, above, main), into(south, below, main)
    from_8 = [into(direct, above, first), into(hop, above, second)]
    from_7 = [into(direct, below, first), into(hop, below, second)]

    def region(act):
        for c in always:
            act(c)

        @pl.when(band == 8)
        def _():
            for c in from_8:
                act(c)

        @pl.when(band != 8)
        def _():
            act(from_north)

        @pl.when(band == 7)
        def _():
            for c in from_7:
                act(c)

        @pl.when(band != 7)
        def _():
            act(from_south)

    region(lambda c: c.start())
    moves = [
        (0, QKV, lambda where: w_ref.at[where], w_sem),
        (QKV, D + FF, lambda where: pu_ref.at[where], pu_sem),
    ]
    for n in range(4):
        moves.append(
            (QKV + D + FF + D * n, D, lambda where, n=n: dn_ref.at[where + (n,)], dn_sem)
        )
    wait_qkv, *waits = place(pos, mine, other, moves)
    fetch.start()

    source = slot_source(lax.broadcasted_iota(jnp.int32, (SPREAD, REGION), 0))
    token = lax.broadcasted_iota(jnp.int32, (SPREAD, REGION), 1) - (STRIP - EDGE)
    spread = jnp.where(source == token, 1.0, 0.0).astype(BF16)
    region(lambda c: c.wait())
    wait_qkv()
    for r in range(REG):
        rows = jnp.dot(spread, reg_ref[r], preferred_element_type=F32).astype(BF16)
        kv = jnp.dot(
            rows, w_ref[:, :, :, :, D:].reshape(D, 2 * D), preferred_element_type=F32
        ).astype(BF16)
        kv_ref[r] = kv.reshape(WINS, LEV, SLOT, 2 * D)
        if HALF <= r < HALF + ROWS:
            q = jnp.dot(
                rows, w_ref[:, :, :, :, 0:D].reshape(D, D), preferred_element_type=F32
            ).astype(BF16)
            q_ref[r - HALF] = (q * jnp.asarray(0.125, BF16)).reshape(WINS, LEV, SLOT, D)

    lane = lax.broadcasted_iota(jnp.int32, (1, 256), 1) // 64

    def window(h, j, levels, half):
        feats = slice(256 * half, 256 * half + 256)
        vals = slice(D + 256 * half, D + 256 * half + 256)
        n_q, n_k = len(levels) * HALF * SLOT, len(levels) * ROWS * SLOT
        q = jnp.concatenate(
            [q_ref[pl.ds(HALF * h, HALF), j, lv, :, feats] for lv in levels], axis=0
        ).reshape(n_q, 256)
        k = jnp.concatenate(
            [kv_ref[pl.ds(ROWS * h, ROWS), j, lv, :, feats] for lv in levels], axis=0
        ).reshape(n_k, 256)
        v = jnp.concatenate(
            [kv_ref[pl.ds(ROWS * h, ROWS), j, lv, :, vals] for lv in levels], axis=0
        ).reshape(n_k, 256)
        key = lax.broadcasted_iota(jnp.int32, (1, n_k), 1)
        key_row = lax.rem(key // SLOT, ROWS)
        first_row = jnp.where(jnp.logical_and(h == 0, band == 0), HALF, 0)
        last_row = jnp.where(jnp.logical_and(h == 1, band == 15), HALF, ROWS)
        bias = jnp.where(lax.rem(key, SLOT) >= 2 * RIM, -jnp.inf, 0.0)
        bias = jnp.where(key_row < first_row, -jnp.inf, bias)
        bias = jnp.where(key_row >= last_row, -jnp.inf, bias)
        packed = jnp.concatenate(
            [jnp.where(lane == hh, q, jnp.zeros_like(q)) for hh in range(4)], axis=0
        )
        s = lax.dot_general(packed, k, (((1,), (1,)), ((), ())), preferred_element_type=F32)
        s = s + bias
        p = jnp.exp(s - jnp.max(s, axis=-1, keepdims=True))
        total = jnp.sum(p, axis=-1, keepdims=True)
        o = jnp.dot(p.astype(BF16), v, preferred_element_type=F32)
        o = o * (1.0 / total)
        result = o[0:n_q]
        for hh in range(1, 4):
            result = jnp.where(lane == hh, o[hh * n_q : (hh + 1) * n_q], result)
        result = result.astype(BF16).reshape(len(levels), HALF, SLOT, 256)
        for n, lv in enumerate(levels):
            att_ref[pl.ds(HALF * h, HALF), j, lv, :, feats] = result[n]

    def attend(n, _):
        h, j = n // WINS, lax.rem(n, WINS)
        for levels in ((1, 2), (0,), (3,)):
            for half in range(2):
                window(h, j, levels, half)
        return 0

    lax.fori_loop(0, 2 * WINS, attend, 0, unroll=8)

    token = lax.broadcasted_iota(jnp.int32, (LINE, SPREAD), 0) + EDGE
    source = slot_source(lax.broadcasted_iota(jnp.int32, (LINE, SPREAD), 1))
    gather = jnp.where(source == token, 1.0, 0.0).astype(BF16)
    waits[0]()
    fetch.wait()
    gain = gain_ref[...]

    def widen(n):
        rows = slice(n * CHUNK_ROWS, (n + 1) * CHUNK_ROWS)
        attended = jnp.concatenate(
            [
                jnp.dot(
                    gather, att_ref[r].reshape(SPREAD, D), preferred_element_type=F32
                ).astype(BF16)
                for r in range(n * CHUNK_ROWS, (n + 1) * CHUNK_ROWS)
            ],
            axis=0,
        )
        residual = tok_ref[rows].astype(F32).reshape(CHUNK_ROWS * LINE, D) + jnp.dot(
            attended, pu_ref[:, :, :, :, 0:D].reshape(D, D), preferred_element_type=F32
        )
        return residual, norm(residual, gain).astype(BF16)

    def hide(normed, f):
        up = jnp.dot(
            normed,
            pu_ref[:, :, :, :, D + D * f : D + D * (f + 1)].reshape(D, D),
            preferred_element_type=F32,
        )
        return (0.5 * up * (1.0 + lax.erf(up * 0.7071067811865476))).astype(BF16)

    for n in range(ROWS // CHUNK_ROWS):
        total, normed = widen(n)
        for f in range(4):
            hidden = hide(normed, f)
            if n == 0 and f == 0:
                for wait in waits[1:]:
                    wait()
            total = total + jnp.dot(
                hidden, dn_ref[f].reshape(D, D), preferred_element_type=F32
            )
        rows = slice(n * CHUNK_ROWS, (n + 1) * CHUNK_ROWS)
        out_ref[rows] = total.reshape(CHUNK_ROWS, COLS, LEV, D).astype(BF16)


def block_call(position, gain, tokens, halo, mine, other):
    return pl.pallas_call(
        functools.partial(block_kernel, position),
        out_shape=jax.ShapeDtypeStruct((ROWS, COLS, LEV, D), BF16),
        in_specs=[whole()] + [anywhere()] * 16,
        out_specs=whole(),
        scratch_shapes=[
            pltpu.VMEM((ROWS, COLS, LEV, D), BF16),
            pltpu.VMEM((REG, REGION, D), BF16),
            pltpu.VMEM((4, 4, 2, 16, QKV), BF16),
            pltpu.VMEM((4, 4, 2, 16, D + FF), BF16),
            pltpu.VMEM((4, 4, 2, 4, 16, D), BF16),
            pltpu.VMEM((ROWS, WINS, LEV, SLOT, D), BF16),
            pltpu.VMEM((REG, WINS, LEV, SLOT, 2 * D), BF16),
            pltpu.VMEM((ROWS, WINS, LEV, SLOT, D), BF16),
        ]
        + [pltpu.SemaphoreType.DMA] * 5,
        compiler_params=pltpu.CompilerParams(vmem_limit_bytes=VMEM),
        name="block",
    )(gain, tokens, *halo, *mine, *other)


AXES = ("yh", "z", "x", "yl", "core")
SIZES = (2, 8, 4, 4, 2)


def number(yh, z, x, yl, core):
    return (((yh * 8 + z) * 4 + x) * 4 + yl) * 2 + core


def each_device():
    for yh in range(2):
        for z in range(8):
            for x in range(4):
                for yl in range(4):
                    for core in range(2):
                        yield yh, z, x, yl, core


def ring_pairs(by, first):
    pairs = []
    for yh, z, x, yl, core in each_device():
        if (core == 0) == first:
            y = yh * 4 + yl
            y = (y + (-by if by == 2 and y % 2 else by)) % 8
            to = number(y // 4, z, x, y % 4, core)
        else:
            to = number(yh, z, (x + by) % 4, yl, core)
        pairs.append((number(yh, z, x, yl, core), to))
    return pairs


def lat_pairs(by):
    pairs = []
    for yh, z, x, yl, core in each_device():
        if 0 <= z + by < 8:
            pairs.append((number(yh, z, x, yl, core), number(yh, z + by, x, yl, core)))
    return pairs


def middle_pairs():
    pairs = []
    for yh, z, x, yl, core in each_device():
        if (yh, z) in ((0, 7), (1, 0)):
            pairs.append((number(yh, z, x, yl, core), number(1 - yh, 7 - z, x, yl, core)))
    return pairs


def hop_pairs():
    pairs = []
    for yh, z, x, yl, core in each_device():
        if (yh, z) in ((0, 7), (1, 0)):
            pairs.append((number(yh, z, x, yl, core), number(yh, 7 - z, x, yl, core)))
    return pairs


def onward_pairs():
    pairs = []
    for yh, z, x, yl, core in each_device():
        if (yh, z) in ((0, 0), (1, 7)):
            pairs.append((number(yh, z, x, yl, core), number(1 - yh, z, x, yl, core)))
    return pairs


def lon_pairs(by):
    pairs = []
    for yh, z, x, yl, core in each_device():
        lon = ((x * 4 + yl) * 2 + core + by) % 32
        pairs.append((number(yh, z, x, yl, core), number(yh, z, lon // 8, lon // 2 % 4, lon % 2)))
    return pairs


def core_pairs():
    return [(number(*d), number(*d[:4], 1 - d[4])) for d in each_device()]


def send(value, pairs):
    return lax.ppermute(value, AXES, pairs)


def gather_stage(block, first):
    return [
        block,
        send(block, ring_pairs(1, first)),
        send(block, ring_pairs(-1, first)),
        send(block, ring_pairs(2, first)),
    ]


def position():
    pos = (lax.axis_index("x"), lax.axis_index("yl"), lax.axis_index("core"))
    return pos, lax.axis_index("yh") * 8 + lax.axis_index("z")


def body(tokens, gain_attn, gain_mlp, w_qkv, w_proj, w_up, w_down):
    (x, y, core), band = position()
    tok = tokens.transpose(1, 2, 0, 3)
    packed, top, low, direct, hop = pack_call(
        position, gain_attn.reshape(1, D), tok, w_qkv, w_proj, w_up, w_down
    )
    direct = send(direct, middle_pairs())
    hop = send(send(hop, hop_pairs()), onward_pairs())
    north = send(low, lat_pairs(1))
    south = send(top, lat_pairs(-1))

    mine, behind, ahead, far = gather_stage(packed, True)
    me = jnp.where(core == 0, y, x)
    ordered = []
    for n in range(4):
        ahead_by = lax.rem(n + 4 - me, 4)
        block = jnp.where(ahead_by == 3, behind, mine)
        block = jnp.where(ahead_by == 1, ahead, block)
        ordered.append(jnp.where(ahead_by == 2, far, block))
    line = lax.optimization_barrier(jnp.stack(ordered))
    behind = send(line, ring_pairs(1, False))
    ahead = send(line, ring_pairs(-1, False))
    to_east, to_west = edge_call(position, top, low, north, south, direct, hop)
    behind, ahead, to_east, to_west = lax.optimization_barrier((behind, ahead, to_east, to_west))
    far = [send(behind[:2], ring_pairs(1, False)), send(ahead[2:], ring_pairs(-1, False))]
    own = [line, behind, ahead, *far]
    west = send(to_east, lon_pairs(1))
    east = send(to_west, lon_pairs(-1))
    far, west, east = lax.optimization_barrier((far, west, east))
    near = send(jnp.concatenate([line, behind, ahead], axis=0), core_pairs())
    rest = send(jnp.concatenate(far, axis=0), core_pairs())

    halo = [top, low, north, south, direct, hop, west, east]
    done = block_call(position, gain_mlp.reshape(1, D), tok, halo, own, [near, rest])
    return done.transpose(2, 0, 1, 3)


def solution(mesh):
    torus = Mesh(mesh.devices.reshape(SIZES), AXES)
    weight = P(("x", "yl", "core"), None)
    grid = P(None, ("yh", "z"), ("x", "yl", "core"), None)
    return jax.shard_map(
        body,
        mesh=torus,
        in_specs=(grid, P(), P(), weight, weight, weight, weight),
        out_specs=grid,
        check_vma=False,
    )
```

time: 139 us -> 115 us (0.83)
  waiting for transfers between devices: 34.1 us -> 20.5 us
  local copies, waits for them, and re-layouts: 12.1 us -> 3.25 us
  Pallas kernels: 28.9 us -> 25.3 us
    ppermute x16, waiting for transfers between devices: 34.1 us -> 20.5 us  [send(): return lax.ppermute(value, AXES, pairs)]
    unnamed x41 -> x30, local copies, waits for them, and re-layouts: 8.3 us -> 3.19 us
    pallas_call x2 -> x3, Pallas kernels: 28.9 us -> 25.3 us  [the longest x1 19.8 us: block_call(): pl.pallas_call(functools.partial(block_kernel, position), out_shape=jax.S...]
    reshape x1 -> x0, local copies, waits for them, and re-layouts: 2.8 us -> none  [body(): return done.reshape(LEV, ROWS, COLS, D)]
  transfers between devices with their start and end apart: 16 -> 16, of which waited for: 7 -> 6; matrix products, arithmetic and copies ran while one was open for 1% -> 1% of each run, Pallas kernels for 11% -> 2%
where the time goes in v2:
time: 115 us; the launch traced here: 114 us
  starting transfers between devices  63 us (55%)
  Pallas kernels  25.3 us (22%)
  waiting for transfers between devices  20.5 us (18%)
  local copies, waits for them, and re-layouts  3.25 us (3%)
  other arithmetic  1.46 us (1%)
    ppermute x16, starting transfers between devices, send(): return lax.ppermute(value, AXES, pairs)  63 us
    ppermute x16, waiting for transfers between devices, send(): return lax.ppermute(value, AXES, pairs)  20.5 us
    pallas_call x1, Pallas kernels, block_call(): pl.pallas_call(functools.partial(block_kernel, position), out_shape=jax.S...  19.8 us
    unnamed x30, local copies, waits for them, and re-layouts  3.19 us
    pallas_call x1, Pallas kernels, pack_call(): pl.pallas_call(functools.partial(pack_kernel, position), out_shape=[jax.S...  3.06 us
    pallas_call x1, Pallas kernels, edge_call(): pl.pallas_call(functools.partial(edge_kernel, position), out_shape=[jax.S...  2.48 us
  transfers between devices with their start and end apart: 16, of which 6 were waited for; matrix products, arithmetic and copies ran while one was open for 1% of the time, Pallas kernels for 2%

profile of v2, /device:TPU:1, one launch (start us, length us, event | category | flops | bytes accessed | tf_op | source)
XLA Modules:
  0.0 114.0 jit_solution(2091983437465323222)
XLA Ops:
  0.0 3.1 %pack.1 = (bf16[16,6144]{1,0:T(8,128)(2,1)}, bf16[3,144,512]{2,1,0:T(8,128)(2,1)}, bf16[3,144,512]{2,1,0:T(8,128)(2,1)}, bf16[3,80,512]{2,1,0:T(8,128)(2,1)}, bf16[3,64,512]{2,1,0:T(8,128)(2,1)}) custom-call(f32[1,512]{1,0:T(1,128)} %bitcast.14, bf16[6,36,4,512]{3,2,1,0:T(4,128)(2,1)} %bitcast.12, bf16[16,1536]{1,0:T(8,128)(2,1)} %qkv_ref.1, ...), custom_call_target="tpu_custom_call" | custom-call | tf_op jit(solution)/shard_map/pack/pallas_call | solution.py:78
  3.1 1.3 %collective-permute-start.3 = (bf16[3,64,512]{2,1,0:T(8,128)(2,1)}, bf16[3,64,512]{2,1,0:T(8,128)(2,1)S(1)}, u32[]{:S(2)}, u32[]{:S(2)}) collective-permute-start(bf16[3,64,512]{2,1,0:T(8,128)(2,1)} %get-tuple-element.23), channel_id=1, source_target_pairs={{224,0},{225,1},{226,2},{227,3},{228,4},{229,5},{230,6},{231,7},{2... | collective-permute-start | bytes 589832 | tf_op jit(solution)/shard_map/ppermute | solution.py:435
  4.3 5.5 %collective-permute-start.5 = (bf16[16,6144]{1,0:T(8,128)(2,1)}, bf16[16,6144]{1,0:T(8,128)(2,1)S(1)}, u32[]{:S(2)}, u32[]{:S(2)}) collective-permute-start(bf16[16,6144]{1,0:T(8,128)(2,1)} %get-tuple-element.24), channel_id=1, source_target_pairs={{0,4},{1,17},{2,262},{3,19},{4,256},{5,21},{6,2},{7,23},{8,12},{9,... | collective-permute-start | bytes 589832 | tf_op jit(solution)/shard_map/ppermute | solution.py:435
  9.8 2.8 %collective-permute-start.6 = (bf16[16,6144]{1,0:T(8,128)(2,1)}, bf16[16,6144]{1,0:T(8,128)(2,1)S(1)}, u32[]{:S(2)}, u32[]{:S(2)}) collective-permute-start(bf16[16,6144]{1,0:T(8,128)(2,1)} %get-tuple-element.24), channel_id=1, source_target_pairs={{0,262},{1,25},{2,0},{3,27},{4,2},{5,29},{6,4},{7,31},{8,270},{9,1... | collective-permute-start | bytes 589832 | tf_op jit(solution)/shard_map/ppermute | solution.py:435
  12.6 2.5 %collective-permute-start.7 = (bf16[16,6144]{1,0:T(8,128)(2,1)}, bf16[16,6144]{1,0:T(8,128)(2,1)S(1)}, u32[]{:S(2)}, u32[]{:S(2)}) collective-permute-start(bf16[16,6144]{1,0:T(8,128)(2,1)} %get-tuple-element.24), channel_id=1, source_target_pairs={{0,2},{1,9},{2,4},{3,11},{4,6},{5,13},{6,256},{7,15},{8,10},{9,17}... | collective-permute-start | bytes 589832 | tf_op jit(solution)/shard_map/ppermute | solution.py:435
  15.1 3.4 %collective-permute-start = (bf16[3,144,512]{2,1,0:T(8,128)(2,1)}, bf16[3,144,512]{2,1,0:T(8,128)(2,1)S(1)}, u32[]{:S(2)}, u32[]{:S(2)}) collective-permute-start(bf16[3,144,512]{2,1,0:T(8,128)(2,1)} %get-tuple-element.21.low_ref.refs_1_), channel_id=1, source_target_pairs={{0,32},{1,33},{2,34},{3,35},{4,36},{5,37},{6,38},{7,39},{8,40},{9,... | collective-permute-start | bytes 1327112 | tf_op jit(solution)/shard_map/ppermute | solution.py:435
  18.6 1.3 %collective-permute-start.1 = (bf16[3,144,512]{2,1,0:T(8,128)(2,1)}, bf16[3,144,512]{2,1,0:T(8,128)(2,1)S(1)}, u32[]{:S(2)}, u32[]{:S(2)}) collective-permute-start(bf16[3,144,512]{2,1,0:T(8,128)(2,1)} %get-tuple-element.20.top_ref.refs_0_), channel_id=1, source_target_pairs={{32,0},{33,1},{34,2},{35,3},{36,4},{37,5},{38,6},{39,7},{40,8},{41... | collective-permute-start | bytes 1327112 | tf_op jit(solution)/shard_map/ppermute | solution.py:435
  19.9 0.7 collective-permute-start.2
  20.6 17.6 %collective-permute-start.4 = (bf16[3,64,512]{2,1,0:T(8,128)(2,1)S(1)}, bf16[3,64,512]{2,1,0:T(8,128)(2,1)S(1)}, u32[]{:S(2)}, u32[]{:S(2)}) collective-permute-start(bf16[3,64,512]{2,1,0:T(8,128)(2,1)S(1)} %collective-permute-done.3), channel_id=1, source_target_pairs={{0,256},{1,257},{2,258},{3,259},{4,260},{5,261},{6,262},{7,263},{8... | collective-permute-start | bytes 589832 | tf_op jit(solution)/shard_map/ppermute | solution.py:435
  38.2 1.0 select_bitcast_fusion.3
  39.4 3.2 %collective-permute-start.8 = (bf16[4,16,6144]{2,1,0:T(8,128)(2,1)S(1)}, bf16[4,16,6144]{2,1,0:T(8,128)(2,1)S(1)}, u32[]{:S(2)}, u32[]{:S(2)}) collective-permute-start(bf16[4,16,6144]{2,1,0:T(8,128)(2,1)S(1)} %pad_maximum_fusion.1.refs_8_), channel_id=1, source_target_pairs={{0,8},{1,3},{2,10},{3,5},{4,12},{5,7},{6,14},{7,257},{8,16},{9,11}... | collective-permute-start | bytes 2359304 | tf_op jit(solution)/shard_map/ppermute | solution.py:435
  42.6 3.3 %collective-permute-start.9 = (bf16[4,16,6144]{2,1,0:T(8,128)(2,1)S(1)}, bf16[4,16,6144]{2,1,0:T(8,128)(2,1)S(1)}, u32[]{:S(2)}, u32[]{:S(2)}) collective-permute-start(bf16[4,16,6144]{2,1,0:T(8,128)(2,1)S(1)} %pad_maximum_fusion.1.refs_8_), channel_id=1, source_target_pairs={{0,24},{1,263},{2,26},{3,1},{4,28},{5,3},{6,30},{7,5},{8,0},{9,271... | collective-permute-start | bytes 2359304 | tf_op jit(solution)/shard_map/ppermute | solution.py:435
  46.0 0.6 copy-done.12
  46.6 0.2 copy-done.7
  46.7 0.8 copy-done.8
  47.5 2.5 %edges.1 = (bf16[12,32,512]{2,1,0:T(8,128)(2,1)}, bf16[12,32,512]{2,1,0:T(8,128)(2,1)}) custom-call(bf16[3,144,512]{2,1,0:T(8,128)(2,1)} %get-tuple-element.20.top_ref.refs_0_, bf16[3,144,512]{2,1,0:T(8,128)(2,1)} %get-tuple-element.21.low_ref.refs_1_, bf16[3,144,512]{2,1,0:T(8,128)(2,1)} %copy-done.7, bf16[3,144,512]{2,1,0:T(8,128)(2,1)} %copy-done.8, ...), custom_call_target="tpu_custom_call" | custom-call | flops 10000000000 | bytes 8388608 | tf_op jit(solution)/shard_map/edges/pallas_call | solution.py:146
  50.0 7.5 %collective-permute-done.8.refs_9_ = bf16[4,16,6144]{2,1,0:T(8,128)(2,1)S(1)} collective-permute-done((bf16[4,16,6144]{2,1,0:T(8,128)(2,1)S(1)}, bf16[4,16,6144]{2,1,0:T(8,128)(2,1)S(1)}, u32[]{:S(2)}, u32[]{:S(2)}) %collective-permute-start.8) | collective-permute-done | bytes 786464 | tf_op jit(solution)/shard_map/ppermute | solution.py:435
  57.4 0.1 collective-permute-done.9.refs_10_
  57.6 0.3 pad_maximum_fusion
  57.9 4.3 %collective-permute-start.14 = (bf16[12,16,6144]{2,1,0:T(8,128)(2,1)S(1)}, bf16[12,16,6144]{2,1,0:T(8,128)(2,1)S(1)}, u32[]{:S(2)}, u32[]{:S(2)}) collective-permute-start(bf16[12,16,6144]{2,1,0:T(8,128)(2,1)S(1)} %pad_maximum_fusion), channel_id=1, source_target_pairs={{0,1},{1,0},{2,3},{3,2},{4,5},{5,4},{6,7},{7,6},{8,9},{9,8},{10,11... | collective-permute-start | bytes 7077896 | tf_op jit(solution)/shard_map/ppermute | solution.py:435
  62.3 3.0 %collective-permute-start.10 = (bf16[2,16,6144]{2,1,0:T(8,128)(2,1)S(1)}, bf16[2,16,6144]{2,1,0:T(8,128)(2,1)S(1)}, u32[]{:S(2)}, u32[]{:S(2)}) collective-permute-start(bf16[2,16,6144]{2,1,0:T(8,128)(2,1)S(1)} %slice.6), channel_id=1, source_target_pairs={{0,8},{1,3},{2,10},{3,5},{4,12},{5,7},{6,14},{7,257},{8,16},{9,11}... | collective-permute-start | bytes 1179656 | tf_op jit(solution)/shard_map/ppermute | solution.py:435
  65.3 4.8 %collective-permute-start.11 = (bf16[2,16,6144]{2,1,0:T(8,128)(2,1)S(1)}, bf16[2,16,6144]{2,1,0:T(8,128)(2,1)S(1)}, u32[]{:S(2)}, u32[]{:S(2)}) collective-permute-start(bf16[2,16,6144]{2,1,0:T(8,128)(2,1)S(1)} %slice.7), channel_id=1, source_target_pairs={{0,24},{1,263},{2,26},{3,1},{4,28},{5,3},{6,30},{7,5},{8,0},{9,271... | collective-permute-start | bytes 1179656 | tf_op jit(solution)/shard_map/ppermute | solution.py:435
  70.1 2.1 %collective-permute-start.12 = (bf16[12,32,512]{2,1,0:T(8,128)(2,1)S(1)}, bf16[12,32,512]{2,1,0:T(8,128)(2,1)S(1)}, u32[]{:S(2)}, u32[]{:S(2)}) collective-permute-start(bf16[12,32,512]{2,1,0:T(8,128)(2,1)S(1)} %copy-done.14), channel_id=1, source_target_pairs={{0,1},{1,2},{2,3},{3,4},{4,5},{5,6},{6,7},{7,8},{8,9},{9,10},{10,1... | collective-permute-start | bytes 1179656 | tf_op jit(solution)/shard_map/ppermute | solution.py:435
  72.3 2.2 %collective-permute-start.13 = (bf16[12,32,512]{2,1,0:T(8,128)(2,1)S(1)}, bf16[12,32,512]{2,1,0:T(8,128)(2,1)S(1)}, u32[]{:S(2)}, u32[]{:S(2)}) collective-permute-start(bf16[12,32,512]{2,1,0:T(8,128)(2,1)S(1)} %copy-done.13), channel_id=1, source_target_pairs={{0,31},{1,0},{2,1},{3,2},{4,3},{5,4},{6,5},{7,6},{8,7},{9,8},{10,9... | collective-permute-start | bytes 1179656 | tf_op jit(solution)/shard_map/ppermute | solution.py:435
  74.5 0.3 collective-permute-done.11.refs_12_
  74.8 2.1 %collective-permute-done.12.refs_6_ = bf16[12,32,512]{2,1,0:T(8,128)(2,1)S(1)} collective-permute-done((bf16[12,32,512]{2,1,0:T(8,128)(2,1)S(1)}, bf16[12,32,512]{2,1,0:T(8,128)(2,1)S(1)}, u32[]{:S(2)}, u32[]{:S(2)}) %collective-permute-start.12) | collective-permute-done | bytes 393248 | tf_op jit(solution)/shard_map/ppermute | solution.py:435
  77.0 8.5 %collective-permute-done.13.refs_7_ = bf16[12,32,512]{2,1,0:T(8,128)(2,1)S(1)} collective-permute-done((bf16[12,32,512]{2,1,0:T(8,128)(2,1)S(1)}, bf16[12,32,512]{2,1,0:T(8,128)(2,1)S(1)}, u32[]{:S(2)}, u32[]{:S(2)}) %collective-permute-start.13) | collective-permute-done | bytes 393248 | tf_op jit(solution)/shard_map/ppermute | solution.py:435
  85.5 5.0 %collective-permute-start.15 = (bf16[4,16,6144]{2,1,0:T(8,128)(2,1)S(1)}, bf16[4,16,6144]{2,1,0:T(8,128)(2,1)S(1)}, u32[]{:S(2)}, u32[]{:S(2)}) collective-permute-start(bf16[4,16,6144]{2,1,0:T(8,128)(2,1)S(1)} %pad_maximum_fusion.2), channel_id=1, source_target_pairs={{0,1},{1,0},{2,3},{3,2},{4,5},{5,4},{6,7},{7,6},{8,9},{9,8},{10,11... | collective-permute-start | bytes 2359304 | tf_op jit(solution)/shard_map/ppermute | solution.py:435
  90.5 1.9 %collective-permute-done.15.refs_14_ = bf16[4,16,6144]{2,1,0:T(8,128)(2,1)S(1)} collective-permute-done((bf16[4,16,6144]{2,1,0:T(8,128)(2,1)S(1)}, bf16[4,16,6144]{2,1,0:T(8,128)(2,1)S(1)}, u32[]{:S(2)}, u32[]{:S(2)}) %collective-permute-start.15) | collective-permute-done | bytes 786464 | tf_op jit(solution)/shard_map/ppermute | solution.py:435
  92.5 0.9 copy-done.6
  93.3 0.7 copy-done.3
  94.1 19.8 %block.1 = bf16[6,36,4,512]{3,2,1,0:T(4,128)(2,1)} custom-call(f32[1,512]{1,0:T(1,128)} %bitcast.15, bf16[6,36,4,512]{3,2,1,0:T(4,128)(2,1)} %bitcast.13, bf16[3,144,512]{2,1,0:T(8,128)(2,1)} %get-tuple-element.20.top_ref.refs_0_, bf16[3,144,512]{2,1,0:T(8,128)(2,1)} %get-tuple-element.21.low_ref.refs_1_, bf16[3,144,512]{2,1,0:T(8,128)(2,1)} %copy-done.7, ...), custom_call_target="tpu_custom_call" | custom-call | tf_op jit(solution)/shard_map/block/pallas_call | solution.py:339
  (39 shorter events, 0.3 us)
Async XLA Ops:
  3.1 15.5 %collective-permute-start.3 = (bf16[3,64,512]{2,1,0:T(8,128)(2,1)}, bf16[3,64,512]{2,1,0:T(8,128)(2,1)S(1)}, u32[]{:S(2)}, u32[]{:S(2)}) collective-permute-start(bf16[3,64,512]{2,1,0:T(8,128)(2,1)} %get-tuple-element.23), channel_id=1, source_target_pairs={{224,0},{225,1},{226,2},{227,3},{228,4},{229,5},{230,6},{231,7},{2... | collective-permute-start | bytes 589832 | tf_op jit(solution)/shard_map/ppermute | solution.py:435
  4.3 15.5 %collective-permute-start.5 = (bf16[16,6144]{1,0:T(8,128)(2,1)}, bf16[16,6144]{1,0:T(8,128)(2,1)S(1)}, u32[]{:S(2)}, u32[]{:S(2)}) collective-permute-start(bf16[16,6144]{1,0:T(8,128)(2,1)} %get-tuple-element.24), channel_id=1, source_target_pairs={{0,4},{1,17},{2,262},{3,19},{4,256},{5,21},{6,2},{7,23},{8,12},{9,... | collective-permute-start | bytes 589832 | tf_op jit(solution)/shard_map/ppermute | solution.py:435
  9.8 10.8 %collective-permute-start.6 = (bf16[16,6144]{1,0:T(8,128)(2,1)}, bf16[16,6144]{1,0:T(8,128)(2,1)S(1)}, u32[]{:S(2)}, u32[]{:S(2)}) collective-permute-start(bf16[16,6144]{1,0:T(8,128)(2,1)} %get-tuple-element.24), channel_id=1, source_target_pairs={{0,262},{1,25},{2,0},{3,27},{4,2},{5,29},{6,4},{7,31},{8,270},{9,1... | collective-permute-start | bytes 589832 | tf_op jit(solution)/shard_map/ppermute | solution.py:435
  12.6 25.6 %collective-permute-start.7 = (bf16[16,6144]{1,0:T(8,128)(2,1)}, bf16[16,6144]{1,0:T(8,128)(2,1)S(1)}, u32[]{:S(2)}, u32[]{:S(2)}) collective-permute-start(bf16[16,6144]{1,0:T(8,128)(2,1)} %get-tuple-element.24), channel_id=1, source_target_pairs={{0,2},{1,9},{2,4},{3,11},{4,6},{5,13},{6,256},{7,15},{8,10},{9,17}... | collective-permute-start | bytes 589832 | tf_op jit(solution)/shard_map/ppermute | solution.py:435
  15.1 30.8 %collective-permute-start = (bf16[3,144,512]{2,1,0:T(8,128)(2,1)}, bf16[3,144,512]{2,1,0:T(8,128)(2,1)S(1)}, u32[]{:S(2)}, u32[]{:S(2)}) collective-permute-start(bf16[3,144,512]{2,1,0:T(8,128)(2,1)} %get-tuple-element.21.low_ref.refs_1_), channel_id=1, source_target_pairs={{0,32},{1,33},{2,34},{3,35},{4,36},{5,37},{6,38},{7,39},{8,40},{9,... | collective-permute-start | bytes 1327112 | tf_op jit(solution)/shard_map/ppermute | solution.py:435
  18.6 27.4 %collective-permute-start.1 = (bf16[3,144,512]{2,1,0:T(8,128)(2,1)}, bf16[3,144,512]{2,1,0:T(8,128)(2,1)S(1)}, u32[]{:S(2)}, u32[]{:S(2)}) collective-permute-start(bf16[3,144,512]{2,1,0:T(8,128)(2,1)} %get-tuple-element.20.top_ref.refs_0_), channel_id=1, source_target_pairs={{32,0},{33,1},{34,2},{35,3},{36,4},{37,5},{38,6},{39,7},{40,8},{41... | collective-permute-start | bytes 1327112 | tf_op jit(solution)/shard_map/ppermute | solution.py:435
  19.9 22.7 %collective-permute-start.2 = (bf16[3,80,512]{2,1,0:T(8,128)(2,1)}, bf16[3,80,512]{2,1,0:T(8,128)(2,1)S(1)}, u32[]{:S(2)}, u32[]{:S(2)}) collective-permute-start(bf16[3,80,512]{2,1,0:T(8,128)(2,1)} %get-tuple-element.22), channel_id=1, source_target_pairs={{224,256},{225,257},{226,258},{227,259},{228,260},{229,261},{230,2... | collective-permute-start | bytes 737288 | tf_op jit(solution)/shard_map/ppermute | solution.py:435
  20.6 25.3 %collective-permute-start.4 = (bf16[3,64,512]{2,1,0:T(8,128)(2,1)S(1)}, bf16[3,64,512]{2,1,0:T(8,128)(2,1)S(1)}, u32[]{:S(2)}, u32[]{:S(2)}) collective-permute-start(bf16[3,64,512]{2,1,0:T(8,128)(2,1)S(1)} %collective-permute-done.3), channel_id=1, source_target_pairs={{0,256},{1,257},{2,258},{3,259},{4,260},{5,261},{6,262},{7,263},{8... | collective-permute-start | bytes 589832 | tf_op jit(solution)/shard_map/ppermute | solution.py:435
  39.4 18.2 %copy-start = (bf16[4,16,6144]{2,1,0:T(8,128)(2,1)}, bf16[4,16,6144]{2,1,0:T(8,128)(2,1)S(1)}, u32[]{:S(2)}) copy-start(bf16[4,16,6144]{2,1,0:T(8,128)(2,1)S(1)} %pad_maximum_fusion.1.refs_8_) | copy-start | bytes 2359300
  39.4 18.1 %collective-permute-start.8 = (bf16[4,16,6144]{2,1,0:T(8,128)(2,1)S(1)}, bf16[4,16,6144]{2,1,0:T(8,128)(2,1)S(1)}, u32[]{:S(2)}, u32[]{:S(2)}) collective-permute-start(bf16[4,16,6144]{2,1,0:T(8,128)(2,1)S(1)} %pad_maximum_fusion.1.refs_8_), channel_id=1, source_target_pairs={{0,8},{1,3},{2,10},{3,5},{4,12},{5,7},{6,14},{7,257},{8,16},{9,11}... | collective-permute-start | bytes 2359304 | tf_op jit(solution)/shard_map/ppermute | solution.py:435
  42.6 3.4 %copy-start.11 = (bf16[3,80,512]{2,1,0:T(8,128)(2,1)}, bf16[3,80,512]{2,1,0:T(8,128)(2,1)S(1)}, u32[]{:S(2)}) copy-start(bf16[3,80,512]{2,1,0:T(8,128)(2,1)S(1)} %collective-permute-done.2.direct_ref.refs_4_) | copy-start | bytes 737284
  42.6 15.0 %collective-permute-start.9 = (bf16[4,16,6144]{2,1,0:T(8,128)(2,1)S(1)}, bf16[4,16,6144]{2,1,0:T(8,128)(2,1)S(1)}, u32[]{:S(2)}, u32[]{:S(2)}) collective-permute-start(bf16[4,16,6144]{2,1,0:T(8,128)(2,1)S(1)} %pad_maximum_fusion.1.refs_8_), channel_id=1, source_target_pairs={{0,24},{1,263},{2,26},{3,1},{4,28},{5,3},{6,30},{7,5},{8,0},{9,271... | collective-permute-start | bytes 2359304 | tf_op jit(solution)/shard_map/ppermute | solution.py:435
  45.9 0.7 copy-start.12
  45.9 0.8 copy-start.7
  46.7 0.8 copy-start.8
  57.4 4.8 %copy-start.1 = (bf16[4,16,6144]{2,1,0:T(8,128)(2,1)}, bf16[4,16,6144]{2,1,0:T(8,128)(2,1)S(1)}, u32[]{:S(2)}) copy-start(bf16[4,16,6144]{2,1,0:T(8,128)(2,1)S(1)} %collective-permute-done.8.refs_9_) | copy-start | bytes 2359300
  57.6 4.7 %copy-start.2 = (bf16[4,16,6144]{2,1,0:T(8,128)(2,1)}, bf16[4,16,6144]{2,1,0:T(8,128)(2,1)S(1)}, u32[]{:S(2)}) copy-start(bf16[4,16,6144]{2,1,0:T(8,128)(2,1)S(1)} %collective-permute-done.9.refs_10_) | copy-start | bytes 2359300
  57.6 12.5 %copy-start.14 = (bf16[12,32,512]{2,1,0:T(8,128)(2,1)S(1)}, bf16[12,32,512]{2,1,0:T(8,128)(2,1)}, u32[]{:S(2)}) copy-start(bf16[12,32,512]{2,1,0:T(8,128)(2,1)} %get-tuple-element.29) | copy-start | bytes 1179652
  57.6 14.7 %copy-start.13 = (bf16[12,32,512]{2,1,0:T(8,128)(2,1)S(1)}, bf16[12,32,512]{2,1,0:T(8,128)(2,1)}, u32[]{:S(2)}) copy-start(bf16[12,32,512]{2,1,0:T(8,128)(2,1)} %get-tuple-element.30) | copy-start | bytes 1179652
  57.9 34.6 %collective-permute-start.14 = (bf16[12,16,6144]{2,1,0:T(8,128)(2,1)S(1)}, bf16[12,16,6144]{2,1,0:T(8,128)(2,1)S(1)}, u32[]{:S(2)}, u32[]{:S(2)}) collective-permute-start(bf16[12,16,6144]{2,1,0:T(8,128)(2,1)S(1)} %pad_maximum_fusion), channel_id=1, source_target_pairs={{0,1},{1,0},{2,3},{3,2},{4,5},{5,4},{6,7},{7,6},{8,9},{9,8},{10,11... | collective-permute-start | bytes 7077896 | tf_op jit(solution)/shard_map/ppermute | solution.py:435
  62.3 12.2 %collective-permute-start.10 = (bf16[2,16,6144]{2,1,0:T(8,128)(2,1)S(1)}, bf16[2,16,6144]{2,1,0:T(8,128)(2,1)S(1)}, u32[]{:S(2)}, u32[]{:S(2)}) collective-permute-start(bf16[2,16,6144]{2,1,0:T(8,128)(2,1)S(1)} %slice.6), channel_id=1, source_target_pairs={{0,8},{1,3},{2,10},{3,5},{4,12},{5,7},{6,14},{7,257},{8,16},{9,11}... | collective-permute-start | bytes 1179656 | tf_op jit(solution)/shard_map/ppermute | solution.py:435
  65.3 9.5 %collective-permute-start.11 = (bf16[2,16,6144]{2,1,0:T(8,128)(2,1)S(1)}, bf16[2,16,6144]{2,1,0:T(8,128)(2,1)S(1)}, u32[]{:S(2)}, u32[]{:S(2)}) collective-permute-start(bf16[2,16,6144]{2,1,0:T(8,128)(2,1)S(1)} %slice.7), channel_id=1, source_target_pairs={{0,24},{1,263},{2,26},{3,1},{4,28},{5,3},{6,30},{7,5},{8,0},{9,271... | collective-permute-start | bytes 1179656 | tf_op jit(solution)/shard_map/ppermute | solution.py:435
  70.1 6.8 %collective-permute-start.12 = (bf16[12,32,512]{2,1,0:T(8,128)(2,1)S(1)}, bf16[12,32,512]{2,1,0:T(8,128)(2,1)S(1)}, u32[]{:S(2)}, u32[]{:S(2)}) collective-permute-start(bf16[12,32,512]{2,1,0:T(8,128)(2,1)S(1)} %copy-done.14), channel_id=1, source_target_pairs={{0,1},{1,2},{2,3},{3,4},{4,5},{5,6},{6,7},{7,8},{8,9},{9,10},{10,1... | collective-permute-start | bytes 1179656 | tf_op jit(solution)/shard_map/ppermute | solution.py:435
  72.3 13.2 %collective-permute-start.13 = (bf16[12,32,512]{2,1,0:T(8,128)(2,1)S(1)}, bf16[12,32,512]{2,1,0:T(8,128)(2,1)S(1)}, u32[]{:S(2)}, u32[]{:S(2)}) collective-permute-start(bf16[12,32,512]{2,1,0:T(8,128)(2,1)S(1)} %copy-done.13), channel_id=1, source_target_pairs={{0,31},{1,0},{2,1},{3,2},{4,3},{5,4},{6,5},{7,6},{8,7},{9,8},{10,9... | collective-permute-start | bytes 1179656 | tf_op jit(solution)/shard_map/ppermute | solution.py:435
  74.5 18.0 %copy-start.4 = (bf16[2,16,6144]{2,1,0:T(8,128)(2,1)}, bf16[2,16,6144]{2,1,0:T(8,128)(2,1)S(1)}, u32[]{:S(2)}) copy-start(bf16[2,16,6144]{2,1,0:T(8,128)(2,1)S(1)} %collective-permute-done.10.refs_11_) | copy-start | bytes 1179652
  74.8 17.6 %copy-start.5 = (bf16[2,16,6144]{2,1,0:T(8,128)(2,1)}, bf16[2,16,6144]{2,1,0:T(8,128)(2,1)S(1)}, u32[]{:S(2)}) copy-start(bf16[2,16,6144]{2,1,0:T(8,128)(2,1)S(1)} %collective-permute-done.11.refs_12_) | copy-start | bytes 1179652
  77.0 15.5 %copy-start.9 = (bf16[12,32,512]{2,1,0:T(8,128)(2,1)}, bf16[12,32,512]{2,1,0:T(8,128)(2,1)S(1)}, u32[]{:S(2)}) copy-start(bf16[12,32,512]{2,1,0:T(8,128)(2,1)S(1)} %collective-permute-done.12.refs_6_) | copy-start | bytes 1179652
  85.5 7.0 %copy-start.10 = (bf16[12,32,512]{2,1,0:T(8,128)(2,1)}, bf16[12,32,512]{2,1,0:T(8,128)(2,1)S(1)}, u32[]{:S(2)}) copy-start(bf16[12,32,512]{2,1,0:T(8,128)(2,1)S(1)} %collective-permute-done.13.refs_7_) | copy-start | bytes 1179652
  85.5 6.9 %collective-permute-start.15 = (bf16[4,16,6144]{2,1,0:T(8,128)(2,1)S(1)}, bf16[4,16,6144]{2,1,0:T(8,128)(2,1)S(1)}, u32[]{:S(2)}, u32[]{:S(2)}) collective-permute-start(bf16[4,16,6144]{2,1,0:T(8,128)(2,1)S(1)} %pad_maximum_fusion.2), channel_id=1, source_target_pairs={{0,1},{1,0},{2,3},{3,2},{4,5},{5,4},{6,7},{7,6},{8,9},{9,8},{10,11... | collective-permute-start | bytes 2359304 | tf_op jit(solution)/shard_map/ppermute | solution.py:435
  92.4 0.9 copy-start.6
  92.4 1.6 %copy-start.3 = (bf16[12,16,6144]{2,1,0:T(8,128)(2,1)}, bf16[12,16,6144]{2,1,0:T(8,128)(2,1)S(1)}, u32[]{:S(2)}) copy-start(bf16[12,16,6144]{2,1,0:T(8,128)(2,1)S(1)} %collective-permute-done.14.refs_13_) | copy-start | bytes 7077892

commit v3 on v2

--- a/solution.py
+++ b/solution.py
@@ -168,15 +168,14 @@
 
 def block_kernel(position, gain_ref, tok_hbm, *refs):
     top, low, north, south, direct, hop, west, east = refs[:8]
-    mine, (near, rest), out_ref = refs[8:13], refs[13:15], refs[15]
-    other = [near.at[0:4], near.at[4:8], near.at[8:12], rest.at[0:2], rest.at[2:4]]
-    tok_ref, reg_ref, w_ref, pu_ref, dn_ref, q_ref, kv_ref, att_ref = refs[16:24]
-    tok_sem, reg_sem, w_sem, pu_sem, dn_sem = refs[24:]
+    mine, other, out_ref = refs[8:13], refs[13:18], refs[18]
+    tok_ref, reg_ref, w_ref, pu_ref, dn_ref, q_ref, kv_ref, att_ref = refs[19:27]
+    tok_sem, reg_sem, w_sem, pu_sem, dn_sem = refs[27:]
     pos, band = position()
     fetch = pltpu.make_async_copy(tok_hbm, tok_ref, tok_sem)
     main = slice(STRIP, STRIP + LINE)
-    first = slice(STRIP, STRIP + DIRECT)
-    second = slice(STRIP + DIRECT, STRIP + LINE)
+    near = slice(STRIP, STRIP + DIRECT)
+    rest = slice(STRIP + DIRECT, STRIP + LINE)
 
     def into(source, rows, cols):
         return pltpu.make_async_copy(source, reg_ref.at[rows, cols], reg_sem)
@@ -189,8 +188,8 @@
         into(east, slice(0, REG), slice(STRIP + LINE, REGION)),
     ]
     from_north, from_south = into(north, above, main), into(south, below, main)
-    from_8 = [into(direct, above, first), into(hop, above, second)]
-    from_7 = [into(direct, below, first), into(hop, below, second)]
+    from_8 = [into(direct, above, near), into(hop, above, rest)]
+    from_7 = [into(direct, below, near), into(hop, below, rest)]
 
     def region(act):
         for c in always:
@@ -339,7 +338,7 @@
     return pl.pallas_call(
         functools.partial(block_kernel, position),
         out_shape=jax.ShapeDtypeStruct((ROWS, COLS, LEV, D), BF16),
-        in_specs=[whole()] + [anywhere()] * 16,
+        in_specs=[whole()] + [anywhere()] * 19,
         out_specs=whole(),
         scratch_shapes=[
             pltpu.VMEM((ROWS, COLS, LEV, D), BF16),
@@ -468,21 +467,18 @@
         block = jnp.where(ahead_by == 3, behind, mine)
         block = jnp.where(ahead_by == 1, ahead, block)
         ordered.append(jnp.where(ahead_by == 2, far, block))
-    line = lax.optimization_barrier(jnp.stack(ordered))
+    line = jnp.stack(ordered)
     behind = send(line, ring_pairs(1, False))
     ahead = send(line, ring_pairs(-1, False))
-    to_east, to_west = edge_call(position, top, low, north, south, direct, hop)
-    behind, ahead, to_east, to_west = lax.optimization_barrier((behind, ahead, to_east, to_west))
     far = [send(behind[:2], ring_pairs(1, False)), send(ahead[2:], ring_pairs(-1, False))]
     own = [line, behind, ahead, *far]
+    other = [send(piece, core_pairs()) for piece in own]
+
+    to_east, to_west = edge_call(position, top, low, north, south, direct, hop)
     west = send(to_east, lon_pairs(1))
     east = send(to_west, lon_pairs(-1))
-    far, west, east = lax.optimization_barrier((far, west, east))
-    near = send(jnp.concatenate([line, behind, ahead], axis=0), core_pairs())
-    rest = send(jnp.concatenate(far, axis=0), core_pairs())
-
     halo = [top, low, north, south, direct, hop, west, east]
-    done = block_call(position, gain_mlp.reshape(1, D), tok, halo, own, [near, rest])
+    done = block_call(position, gain_mlp.reshape(1, D), tok, halo, own, other)
     return done.transpose(2, 0, 1, 3)
 
 

time: 115 us -> 104 us (0.904)
  waiting for transfers between devices: 20.5 us -> 6.56 us
  starting transfers between devices: 63 us -> 66.6 us
    ppermute x16 -> x19, waiting for transfers between devices: 20.5 us -> 6.56 us  [send(): return lax.ppermute(value, AXES, pairs)]
    ppermute x16 -> x19, starting transfers between devices: 63 us -> 66.6 us  [send(): return lax.ppermute(value, AXES, pairs)]
    unnamed x30 -> x32, local copies, waits for them, and re-layouts: 3.19 us -> 2.62 us
  transfers between devices with their start and end apart: 16 -> 19, of which waited for: 6 -> 4; matrix products, arithmetic and copies ran while one was open for 1% -> 1% of each run, Pallas kernels for 2% -> 2%
where the time goes in v3:
time: 104 us; the launch traced here: 103 us
  starting transfers between devices  66.6 us (64%)
  Pallas kernels  25.3 us (24%)
  waiting for transfers between devices  6.56 us (6%)
  local copies, waits for them, and re-layouts  2.67 us (3%)
  other arithmetic  1.13 us (1%)
    ppermute x19, starting transfers between devices, send(): return lax.ppermute(value, AXES, pairs)  66.6 us
    pallas_call x1, Pallas kernels, block_call(): pl.pallas_call(functools.partial(block_kernel, position), out_shape=jax.S...  19.8 us
    ppermute x19, waiting for transfers between devices, send(): return lax.ppermute(value, AXES, pairs)  6.56 us
    pallas_call x1, Pallas kernels, pack_call(): pl.pallas_call(functools.partial(pack_kernel, position), out_shape=[jax.S...  3.06 us
    unnamed x32, local copies, waits for them, and re-layouts  2.62 us
    pallas_call x1, Pallas kernels, edge_call(): pl.pallas_call(functools.partial(edge_kernel, position), out_shape=[jax.S...  2.49 us
  transfers between devices with their start and end apart: 19, of which 4 were waited for; matrix products, arithmetic and copies ran while one was open for 1% of the time, Pallas kernels for 2%

profile of v3, /device:TPU:1, one launch (start us, length us, event | category | flops | bytes accessed | tf_op | source)
XLA Modules:
  0.0 102.9 jit_solution(18400983004453530745)
XLA Ops:
  0.0 3.1 %pack.1 = (bf16[16,6144]{1,0:T(8,128)(2,1)}, bf16[3,144,512]{2,1,0:T(8,128)(2,1)}, bf16[3,144,512]{2,1,0:T(8,128)(2,1)}, bf16[3,80,512]{2,1,0:T(8,128)(2,1)}, bf16[3,64,512]{2,1,0:T(8,128)(2,1)}) custom-call(f32[1,512]{1,0:T(1,128)} %bitcast.14, bf16[6,36,4,512]{3,2,1,0:T(4,128)(2,1)} %bitcast.12, bf16[16,1536]{1,0:T(8,128)(2,1)} %qkv_ref.1, ...), custom_call_target="tpu_custom_call" | custom-call | tf_op jit(solution)/shard_map/pack/pallas_call | solution.py:78
  3.1 1.3 %collective-permute-start.3 = (bf16[3,64,512]{2,1,0:T(8,128)(2,1)}, bf16[3,64,512]{2,1,0:T(8,128)(2,1)S(1)}, u32[]{:S(2)}, u32[]{:S(2)}) collective-permute-start(bf16[3,64,512]{2,1,0:T(8,128)(2,1)} %get-tuple-element.15), channel_id=1, source_target_pairs={{224,0},{225,1},{226,2},{227,3},{228,4},{229,5},{230,6},{231,7},{2... | collective-permute-start | bytes 589832 | tf_op jit(solution)/shard_map/ppermute | solution.py:434
  4.3 3.9 %collective-permute-start.9 = (bf16[16,6144]{1,0:T(8,128)(2,1)}, bf16[16,6144]{1,0:T(8,128)(2,1)S(1)}, u32[]{:S(2)}, u32[]{:S(2)}) collective-permute-start(bf16[16,6144]{1,0:T(8,128)(2,1)} %get-tuple-element.18), channel_id=1, source_target_pairs={{0,2},{1,9},{2,4},{3,11},{4,6},{5,13},{6,256},{7,15},{8,10},{9,17}... | collective-permute-start | bytes 589832 | tf_op jit(solution)/shard_map/ppermute | solution.py:434
  8.3 3.2 %collective-permute-start.8 = (bf16[16,6144]{1,0:T(8,128)(2,1)}, bf16[16,6144]{1,0:T(8,128)(2,1)S(1)}, u32[]{:S(2)}, u32[]{:S(2)}) collective-permute-start(bf16[16,6144]{1,0:T(8,128)(2,1)} %get-tuple-element.18), channel_id=1, source_target_pairs={{0,262},{1,25},{2,0},{3,27},{4,2},{5,29},{6,4},{7,31},{8,270},{9,1... | collective-permute-start | bytes 589832 | tf_op jit(solution)/shard_map/ppermute | solution.py:434
  11.5 3.6 %collective-permute-start.7 = (bf16[16,6144]{1,0:T(8,128)(2,1)}, bf16[16,6144]{1,0:T(8,128)(2,1)S(1)}, u32[]{:S(2)}, u32[]{:S(2)}) collective-permute-start(bf16[16,6144]{1,0:T(8,128)(2,1)} %get-tuple-element.18), channel_id=1, source_target_pairs={{0,4},{1,17},{2,262},{3,19},{4,256},{5,21},{6,2},{7,23},{8,12},{9,... | collective-permute-start | bytes 589832 | tf_op jit(solution)/shard_map/ppermute | solution.py:434
  15.1 0.7 collective-permute-start.2
  15.9 2.7 %collective-permute-done.3 = bf16[3,64,512]{2,1,0:T(8,128)(2,1)S(1)} collective-permute-done((bf16[3,64,512]{2,1,0:T(8,128)(2,1)}, bf16[3,64,512]{2,1,0:T(8,128)(2,1)S(1)}, u32[]{:S(2)}, u32[]{:S(2)}) %collective-permute-start.3) | collective-permute-done | bytes 196640 | tf_op jit(solution)/shard_map/ppermute | solution.py:434
  18.5 1.3 %collective-permute-start.1 = (bf16[3,144,512]{2,1,0:T(8,128)(2,1)}, bf16[3,144,512]{2,1,0:T(8,128)(2,1)S(1)}, u32[]{:S(2)}, u32[]{:S(2)}) collective-permute-start(bf16[3,144,512]{2,1,0:T(8,128)(2,1)} %get-tuple-element.12.top_ref.refs_0_), channel_id=1, source_target_pairs={{32,0},{33,1},{34,2},{35,3},{36,4},{37,5},{38,6},{39,7},{40,8},{41... | collective-permute-start | bytes 1327112 | tf_op jit(solution)/shard_map/ppermute | solution.py:434
  19.8 4.0 %collective-permute-start = (bf16[3,144,512]{2,1,0:T(8,128)(2,1)}, bf16[3,144,512]{2,1,0:T(8,128)(2,1)S(1)}, u32[]{:S(2)}, u32[]{:S(2)}) collective-permute-start(bf16[3,144,512]{2,1,0:T(8,128)(2,1)} %get-tuple-element.13.low_ref.refs_1_), channel_id=1, source_target_pairs={{0,32},{1,33},{2,34},{3,35},{4,36},{5,37},{6,38},{7,39},{8,40},{9,... | collective-permute-start | bytes 1327112 | tf_op jit(solution)/shard_map/ppermute | solution.py:434
  23.9 15.4 %collective-permute-start.4 = (bf16[3,64,512]{2,1,0:T(8,128)(2,1)S(1)}, bf16[3,64,512]{2,1,0:T(8,128)(2,1)S(1)}, u32[]{:S(2)}, u32[]{:S(2)}) collective-permute-start(bf16[3,64,512]{2,1,0:T(8,128)(2,1)S(1)} %collective-permute-done.3), channel_id=1, source_target_pairs={{0,256},{1,257},{2,258},{3,259},{4,260},{5,261},{6,262},{7,263},{8... | collective-permute-start | bytes 589832 | tf_op jit(solution)/shard_map/ppermute | solution.py:434
  39.3 1.0 select_bitcast_fusion.3
  40.5 1.9 %collective-permute-start.11 = (bf16[4,16,6144]{2,1,0:T(8,128)(2,1)S(1)}, bf16[4,16,6144]{2,1,0:T(8,128)(2,1)S(1)}, u32[]{:S(2)}, u32[]{:S(2)}) collective-permute-start(bf16[4,16,6144]{2,1,0:T(8,128)(2,1)S(1)} %pad_maximum_fusion.refs_8_), channel_id=1, source_target_pairs={{0,24},{1,263},{2,26},{3,1},{4,28},{5,3},{6,30},{7,5},{8,0},{9,271... | collective-permute-start | bytes 2359304 | tf_op jit(solution)/shard_map/ppermute | solution.py:434
  42.4 3.4 %collective-permute-start.10 = (bf16[4,16,6144]{2,1,0:T(8,128)(2,1)S(1)}, bf16[4,16,6144]{2,1,0:T(8,128)(2,1)S(1)}, u32[]{:S(2)}, u32[]{:S(2)}) collective-permute-start(bf16[4,16,6144]{2,1,0:T(8,128)(2,1)S(1)} %pad_maximum_fusion.refs_8_), channel_id=1, source_target_pairs={{0,8},{1,3},{2,10},{3,5},{4,12},{5,7},{6,14},{7,257},{8,16},{9,11}... | collective-permute-start | bytes 2359304 | tf_op jit(solution)/shard_map/ppermute | solution.py:434
  45.8 0.4 collective-permute-done.4.hop_ref.refs_5_
  46.2 0.7 copy-done.15
  46.9 0.1 copy-done.6
  47.0 0.8 copy-done.7
  47.8 2.5 %edges.1 = (bf16[12,32,512]{2,1,0:T(8,128)(2,1)}, bf16[12,32,512]{2,1,0:T(8,128)(2,1)}) custom-call(bf16[3,144,512]{2,1,0:T(8,128)(2,1)} %get-tuple-element.12.top_ref.refs_0_, bf16[3,144,512]{2,1,0:T(8,128)(2,1)} %get-tuple-element.13.low_ref.refs_1_, bf16[3,144,512]{2,1,0:T(8,128)(2,1)} %copy-done.7, bf16[3,144,512]{2,1,0:T(8,128)(2,1)} %copy-done.6, ...), custom_call_target="tpu_custom_call" | custom-call | flops 10000000000 | bytes 8388608 | tf_op jit(solution)/shard_map/edges/pallas_call | solution.py:146
  50.3 6.5 %collective-permute-start.5 = (bf16[12,32,512]{2,1,0:T(8,128)(2,1)}, bf16[12,32,512]{2,1,0:T(8,128)(2,1)S(1)}, u32[]{:S(2)}, u32[]{:S(2)}) collective-permute-start(bf16[12,32,512]{2,1,0:T(8,128)(2,1)} %get-tuple-element.16), channel_id=1, source_target_pairs={{0,1},{1,2},{2,3},{3,4},{4,5},{5,6},{6,7},{7,8},{8,9},{9,10},{10,1... | collective-permute-start | bytes 1179656 | tf_op jit(solution)/shard_map/ppermute | solution.py:434
  56.8 1.9 %collective-permute-start.6 = (bf16[12,32,512]{2,1,0:T(8,128)(2,1)}, bf16[12,32,512]{2,1,0:T(8,128)(2,1)S(1)}, u32[]{:S(2)}, u32[]{:S(2)}) collective-permute-start(bf16[12,32,512]{2,1,0:T(8,128)(2,1)} %get-tuple-element.17), channel_id=1, source_target_pairs={{0,31},{1,0},{2,1},{3,2},{4,3},{5,4},{6,5},{7,6},{8,7},{9,8},{10,9... | collective-permute-start | bytes 1179656 | tf_op jit(solution)/shard_map/ppermute | solution.py:434
  58.8 4.9 %collective-permute-start.14 = (bf16[4,16,6144]{2,1,0:T(8,128)(2,1)S(1)}, bf16[4,16,6144]{2,1,0:T(8,128)(2,1)S(1)}, u32[]{:S(2)}, u32[]{:S(2)}) collective-permute-start(bf16[4,16,6144]{2,1,0:T(8,128)(2,1)S(1)} %pad_maximum_fusion.refs_8_), channel_id=1, source_target_pairs={{0,1},{1,0},{2,3},{3,2},{4,5},{5,4},{6,7},{7,6},{8,9},{9,8},{10,11... | collective-permute-start | bytes 2359304 | tf_op jit(solution)/shard_map/ppermute | solution.py:434
  63.8 2.3 %collective-permute-start.13 = (bf16[2,16,6144]{2,1,0:T(8,128)(2,1)S(1)}, bf16[2,16,6144]{2,1,0:T(8,128)(2,1)S(1)}, u32[]{:S(2)}, u32[]{:S(2)}) collective-permute-start(bf16[2,16,6144]{2,1,0:T(8,128)(2,1)S(1)} %slice.9), channel_id=1, source_target_pairs={{0,24},{1,263},{2,26},{3,1},{4,28},{5,3},{6,30},{7,5},{8,0},{9,271... | collective-permute-start | bytes 1179656 | tf_op jit(solution)/shard_map/ppermute | solution.py:434
  66.1 3.0 %collective-permute-start.12 = (bf16[2,16,6144]{2,1,0:T(8,128)(2,1)S(1)}, bf16[2,16,6144]{2,1,0:T(8,128)(2,1)S(1)}, u32[]{:S(2)}, u32[]{:S(2)}) collective-permute-start(bf16[2,16,6144]{2,1,0:T(8,128)(2,1)S(1)} %slice.8), channel_id=1, source_target_pairs={{0,8},{1,3},{2,10},{3,5},{4,12},{5,7},{6,14},{7,257},{8,16},{9,11}... | collective-permute-start | bytes 1179656 | tf_op jit(solution)/shard_map/ppermute | solution.py:434
  69.2 2.5 %collective-permute-start.16 = (bf16[4,16,6144]{2,1,0:T(8,128)(2,1)S(1)}, bf16[4,16,6144]{2,1,0:T(8,128)(2,1)S(1)}, u32[]{:S(2)}, u32[]{:S(2)}) collective-permute-start(bf16[4,16,6144]{2,1,0:T(8,128)(2,1)S(1)} %collective-permute-done.11.refs_10_), channel_id=1, source_target_pairs={{0,1},{1,0},{2,3},{3,2},{4,5},{5,4},{6,7},{7,6},{8,9},{9,8},{10,11... | collective-permute-start | bytes 2359304 | tf_op jit(solution)/shard_map/ppermute | solution.py:434
  71.7 1.9 %collective-permute-start.15 = (bf16[4,16,6144]{2,1,0:T(8,128)(2,1)S(1)}, bf16[4,16,6144]{2,1,0:T(8,128)(2,1)S(1)}, u32[]{:S(2)}, u32[]{:S(2)}) collective-permute-start(bf16[4,16,6144]{2,1,0:T(8,128)(2,1)S(1)} %collective-permute-done.10.refs_9_), channel_id=1, source_target_pairs={{0,1},{1,0},{2,3},{3,2},{4,5},{5,4},{6,7},{7,6},{8,9},{9,8},{10,11... | collective-permute-start | bytes 2359304 | tf_op jit(solution)/shard_map/ppermute | solution.py:434
  73.6 2.4 %collective-permute-start.18 = (bf16[2,16,6144]{2,1,0:T(8,128)(2,1)S(1)}, bf16[2,16,6144]{2,1,0:T(8,128)(2,1)S(1)}, u32[]{:S(2)}, u32[]{:S(2)}) collective-permute-start(bf16[2,16,6144]{2,1,0:T(8,128)(2,1)S(1)} %collective-permute-done.13.refs_12_), channel_id=1, source_target_pairs={{0,1},{1,0},{2,3},{3,2},{4,5},{5,4},{6,7},{7,6},{8,9},{9,8},{10,11... | collective-permute-start | bytes 1179656 | tf_op jit(solution)/shard_map/ppermute | solution.py:434
  76.0 2.2 %collective-permute-done.12.refs_11_ = bf16[2,16,6144]{2,1,0:T(8,128)(2,1)S(1)} collective-permute-done((bf16[2,16,6144]{2,1,0:T(8,128)(2,1)S(1)}, bf16[2,16,6144]{2,1,0:T(8,128)(2,1)S(1)}, u32[]{:S(2)}, u32[]{:S(2)}) %collective-permute-start.12) | collective-permute-done | bytes 393248 | tf_op jit(solution)/shard_map/ppermute | solution.py:434
  78.2 2.4 %collective-permute-start.17 = (bf16[2,16,6144]{2,1,0:T(8,128)(2,1)S(1)}, bf16[2,16,6144]{2,1,0:T(8,128)(2,1)S(1)}, u32[]{:S(2)}, u32[]{:S(2)}) collective-permute-start(bf16[2,16,6144]{2,1,0:T(8,128)(2,1)S(1)} %collective-permute-done.12.refs_11_), channel_id=1, source_target_pairs={{0,1},{1,0},{2,3},{3,2},{4,5},{5,4},{6,7},{7,6},{8,9},{9,8},{10,11... | collective-permute-start | bytes 1179656 | tf_op jit(solution)/shard_map/ppermute | solution.py:434
  80.6 1.3 %collective-permute-done.17.refs_16_ = bf16[2,16,6144]{2,1,0:T(8,128)(2,1)S(1)} collective-permute-done((bf16[2,16,6144]{2,1,0:T(8,128)(2,1)S(1)}, bf16[2,16,6144]{2,1,0:T(8,128)(2,1)S(1)}, u32[]{:S(2)}, u32[]{:S(2)}) %collective-permute-start.17) | collective-permute-done | bytes 393248 | tf_op jit(solution)/shard_map/ppermute | solution.py:434
  82.0 0.7 copy-done.13
  82.7 0.3 copy-done.5
  82.9 19.8 %block.1 = bf16[6,36,4,512]{3,2,1,0:T(4,128)(2,1)} custom-call(f32[1,512]{1,0:T(1,128)} %bitcast.15, bf16[6,36,4,512]{3,2,1,0:T(4,128)(2,1)} %bitcast.13, bf16[3,144,512]{2,1,0:T(8,128)(2,1)} %get-tuple-element.12.top_ref.refs_0_, bf16[3,144,512]{2,1,0:T(8,128)(2,1)} %get-tuple-element.13.low_ref.refs_1_, bf16[3,144,512]{2,1,0:T(8,128)(2,1)} %copy-done.7, ...), custom_call_target="tpu_custom_call" | custom-call | tf_op jit(solution)/shard_map/block/pallas_call | solution.py:338
  (45 shorter events, 0.3 us)
Async XLA Ops:
  3.1 15.5 %collective-permute-start.3 = (bf16[3,64,512]{2,1,0:T(8,128)(2,1)}, bf16[3,64,512]{2,1,0:T(8,128)(2,1)S(1)}, u32[]{:S(2)}, u32[]{:S(2)}) collective-permute-start(bf16[3,64,512]{2,1,0:T(8,128)(2,1)} %get-tuple-element.15), channel_id=1, source_target_pairs={{224,0},{225,1},{226,2},{227,3},{228,4},{229,5},{230,6},{231,7},{2... | collective-permute-start | bytes 589832 | tf_op jit(solution)/shard_map/ppermute | solution.py:434
  4.3 15.5 %collective-permute-start.9 = (bf16[16,6144]{1,0:T(8,128)(2,1)}, bf16[16,6144]{1,0:T(8,128)(2,1)S(1)}, u32[]{:S(2)}, u32[]{:S(2)}) collective-permute-start(bf16[16,6144]{1,0:T(8,128)(2,1)} %get-tuple-element.18), channel_id=1, source_target_pairs={{0,2},{1,9},{2,4},{3,11},{4,6},{5,13},{6,256},{7,15},{8,10},{9,17}... | collective-permute-start | bytes 589832 | tf_op jit(solution)/shard_map/ppermute | solution.py:434
  8.3 15.5 %collective-permute-start.8 = (bf16[16,6144]{1,0:T(8,128)(2,1)}, bf16[16,6144]{1,0:T(8,128)(2,1)S(1)}, u32[]{:S(2)}, u32[]{:S(2)}) collective-permute-start(bf16[16,6144]{1,0:T(8,128)(2,1)} %get-tuple-element.18), channel_id=1, source_target_pairs={{0,262},{1,25},{2,0},{3,27},{4,2},{5,29},{6,4},{7,31},{8,270},{9,1... | collective-permute-start | bytes 589832 | tf_op jit(solution)/shard_map/ppermute | solution.py:434
  11.5 27.8 %collective-permute-start.7 = (bf16[16,6144]{1,0:T(8,128)(2,1)}, bf16[16,6144]{1,0:T(8,128)(2,1)S(1)}, u32[]{:S(2)}, u32[]{:S(2)}) collective-permute-start(bf16[16,6144]{1,0:T(8,128)(2,1)} %get-tuple-element.18), channel_id=1, source_target_pairs={{0,4},{1,17},{2,262},{3,19},{4,256},{5,21},{6,2},{7,23},{8,12},{9,... | collective-permute-start | bytes 589832 | tf_op jit(solution)/shard_map/ppermute | solution.py:434
  15.1 27.3 %collective-permute-start.2 = (bf16[3,80,512]{2,1,0:T(8,128)(2,1)}, bf16[3,80,512]{2,1,0:T(8,128)(2,1)S(1)}, u32[]{:S(2)}, u32[]{:S(2)}) collective-permute-start(bf16[3,80,512]{2,1,0:T(8,128)(2,1)} %get-tuple-element.14), channel_id=1, source_target_pairs={{224,256},{225,257},{226,258},{227,259},{228,260},{229,261},{230,2... | collective-permute-start | bytes 737288 | tf_op jit(solution)/shard_map/ppermute | solution.py:434
  18.5 27.7 %collective-permute-start.1 = (bf16[3,144,512]{2,1,0:T(8,128)(2,1)}, bf16[3,144,512]{2,1,0:T(8,128)(2,1)S(1)}, u32[]{:S(2)}, u32[]{:S(2)}) collective-permute-start(bf16[3,144,512]{2,1,0:T(8,128)(2,1)} %get-tuple-element.12.top_ref.refs_0_), channel_id=1, source_target_pairs={{32,0},{33,1},{34,2},{35,3},{36,4},{37,5},{38,6},{39,7},{40,8},{41... | collective-permute-start | bytes 1327112 | tf_op jit(solution)/shard_map/ppermute | solution.py:434
  19.8 26.4 %collective-permute-start = (bf16[3,144,512]{2,1,0:T(8,128)(2,1)}, bf16[3,144,512]{2,1,0:T(8,128)(2,1)S(1)}, u32[]{:S(2)}, u32[]{:S(2)}) collective-permute-start(bf16[3,144,512]{2,1,0:T(8,128)(2,1)} %get-tuple-element.13.low_ref.refs_1_), channel_id=1, source_target_pairs={{0,32},{1,33},{2,34},{3,35},{4,36},{5,37},{6,38},{7,39},{8,40},{9,... | collective-permute-start | bytes 1327112 | tf_op jit(solution)/shard_map/ppermute | solution.py:434
  23.9 22.3 %collective-permute-start.4 = (bf16[3,64,512]{2,1,0:T(8,128)(2,1)S(1)}, bf16[3,64,512]{2,1,0:T(8,128)(2,1)S(1)}, u32[]{:S(2)}, u32[]{:S(2)}) collective-permute-start(bf16[3,64,512]{2,1,0:T(8,128)(2,1)S(1)} %collective-permute-done.3), channel_id=1, source_target_pairs={{0,256},{1,257},{2,258},{3,259},{4,260},{5,261},{6,262},{7,263},{8... | collective-permute-start | bytes 589832 | tf_op jit(solution)/shard_map/ppermute | solution.py:434
  40.5 18.3 %copy-start = (bf16[4,16,6144]{2,1,0:T(8,128)(2,1)}, bf16[4,16,6144]{2,1,0:T(8,128)(2,1)S(1)}, u32[]{:S(2)}) copy-start(bf16[4,16,6144]{2,1,0:T(8,128)(2,1)S(1)} %pad_maximum_fusion.refs_8_) | copy-start | bytes 2359300
  40.5 23.3 %collective-permute-start.11 = (bf16[4,16,6144]{2,1,0:T(8,128)(2,1)S(1)}, bf16[4,16,6144]{2,1,0:T(8,128)(2,1)S(1)}, u32[]{:S(2)}, u32[]{:S(2)}) collective-permute-start(bf16[4,16,6144]{2,1,0:T(8,128)(2,1)S(1)} %pad_maximum_fusion.refs_8_), channel_id=1, source_target_pairs={{0,24},{1,263},{2,26},{3,1},{4,28},{5,3},{6,30},{7,5},{8,0},{9,271... | collective-permute-start | bytes 2359304 | tf_op jit(solution)/shard_map/ppermute | solution.py:434
  42.4 3.8 %copy-start.14 = (bf16[3,80,512]{2,1,0:T(8,128)(2,1)}, bf16[3,80,512]{2,1,0:T(8,128)(2,1)S(1)}, u32[]{:S(2)}) copy-start(bf16[3,80,512]{2,1,0:T(8,128)(2,1)S(1)} %collective-permute-done.2.direct_ref.refs_4_) | copy-start | bytes 737284
  42.4 23.6 %collective-permute-start.10 = (bf16[4,16,6144]{2,1,0:T(8,128)(2,1)S(1)}, bf16[4,16,6144]{2,1,0:T(8,128)(2,1)S(1)}, u32[]{:S(2)}, u32[]{:S(2)}) collective-permute-start(bf16[4,16,6144]{2,1,0:T(8,128)(2,1)S(1)} %pad_maximum_fusion.refs_8_), channel_id=1, source_target_pairs={{0,8},{1,3},{2,10},{3,5},{4,12},{5,7},{6,14},{7,257},{8,16},{9,11}... | collective-permute-start | bytes 2359304 | tf_op jit(solution)/shard_map/ppermute | solution.py:434
  46.2 0.8 copy-start.6
  50.3 18.8 %collective-permute-start.5 = (bf16[12,32,512]{2,1,0:T(8,128)(2,1)}, bf16[12,32,512]{2,1,0:T(8,128)(2,1)S(1)}, u32[]{:S(2)}, u32[]{:S(2)}) collective-permute-start(bf16[12,32,512]{2,1,0:T(8,128)(2,1)} %get-tuple-element.16), channel_id=1, source_target_pairs={{0,1},{1,2},{2,3},{3,4},{4,5},{5,6},{6,7},{7,8},{8,9},{9,10},{10,1... | collective-permute-start | bytes 1179656 | tf_op jit(solution)/shard_map/ppermute | solution.py:434
  56.8 14.8 %collective-permute-start.6 = (bf16[12,32,512]{2,1,0:T(8,128)(2,1)}, bf16[12,32,512]{2,1,0:T(8,128)(2,1)S(1)}, u32[]{:S(2)}, u32[]{:S(2)}) collective-permute-start(bf16[12,32,512]{2,1,0:T(8,128)(2,1)} %get-tuple-element.17), channel_id=1, source_target_pairs={{0,31},{1,0},{2,1},{3,2},{4,3},{5,4},{6,5},{7,6},{8,7},{9,8},{10,9... | collective-permute-start | bytes 1179656 | tf_op jit(solution)/shard_map/ppermute | solution.py:434
  58.8 21.8 %collective-permute-start.14 = (bf16[4,16,6144]{2,1,0:T(8,128)(2,1)S(1)}, bf16[4,16,6144]{2,1,0:T(8,128)(2,1)S(1)}, u32[]{:S(2)}, u32[]{:S(2)}) collective-permute-start(bf16[4,16,6144]{2,1,0:T(8,128)(2,1)S(1)} %pad_maximum_fusion.refs_8_), channel_id=1, source_target_pairs={{0,1},{1,0},{2,3},{3,2},{4,5},{5,4},{6,7},{7,6},{8,9},{9,8},{10,11... | collective-permute-start | bytes 2359304 | tf_op jit(solution)/shard_map/ppermute | solution.py:434
  63.7 5.4 %copy-start.1 = (bf16[4,16,6144]{2,1,0:T(8,128)(2,1)}, bf16[4,16,6144]{2,1,0:T(8,128)(2,1)S(1)}, u32[]{:S(2)}) copy-start(bf16[4,16,6144]{2,1,0:T(8,128)(2,1)S(1)} %collective-permute-done.11.refs_10_) | copy-start | bytes 2359300
  63.8 9.8 %collective-permute-start.13 = (bf16[2,16,6144]{2,1,0:T(8,128)(2,1)S(1)}, bf16[2,16,6144]{2,1,0:T(8,128)(2,1)S(1)}, u32[]{:S(2)}, u32[]{:S(2)}) collective-permute-start(bf16[2,16,6144]{2,1,0:T(8,128)(2,1)S(1)} %slice.9), channel_id=1, source_target_pairs={{0,24},{1,263},{2,26},{3,1},{4,28},{5,3},{6,30},{7,5},{8,0},{9,271... | collective-permute-start | bytes 1179656 | tf_op jit(solution)/shard_map/ppermute | solution.py:434
  66.1 15.8 %copy-start.2 = (bf16[4,16,6144]{2,1,0:T(8,128)(2,1)}, bf16[4,16,6144]{2,1,0:T(8,128)(2,1)S(1)}, u32[]{:S(2)}) copy-start(bf16[4,16,6144]{2,1,0:T(8,128)(2,1)S(1)} %collective-permute-done.10.refs_9_) | copy-start | bytes 2359300
  66.1 12.1 %collective-permute-start.12 = (bf16[2,16,6144]{2,1,0:T(8,128)(2,1)S(1)}, bf16[2,16,6144]{2,1,0:T(8,128)(2,1)S(1)}, u32[]{:S(2)}, u32[]{:S(2)}) collective-permute-start(bf16[2,16,6144]{2,1,0:T(8,128)(2,1)S(1)} %slice.8), channel_id=1, source_target_pairs={{0,8},{1,3},{2,10},{3,5},{4,12},{5,7},{6,14},{7,257},{8,16},{9,11}... | collective-permute-start | bytes 1179656 | tf_op jit(solution)/shard_map/ppermute | solution.py:434
  69.2 12.8 %copy-start.8 = (bf16[12,32,512]{2,1,0:T(8,128)(2,1)}, bf16[12,32,512]{2,1,0:T(8,128)(2,1)S(1)}, u32[]{:S(2)}) copy-start(bf16[12,32,512]{2,1,0:T(8,128)(2,1)S(1)} %collective-permute-done.5.refs_6_) | copy-start | bytes 1179652
  69.2 11.4 %collective-permute-start.16 = (bf16[4,16,6144]{2,1,0:T(8,128)(2,1)S(1)}, bf16[4,16,6144]{2,1,0:T(8,128)(2,1)S(1)}, u32[]{:S(2)}, u32[]{:S(2)}) collective-permute-start(bf16[4,16,6144]{2,1,0:T(8,128)(2,1)S(1)} %collective-permute-done.11.refs_10_), channel_id=1, source_target_pairs={{0,1},{1,0},{2,3},{3,2},{4,5},{5,4},{6,7},{7,6},{8,9},{9,8},{10,11... | collective-permute-start | bytes 2359304 | tf_op jit(solution)/shard_map/ppermute | solution.py:434
  71.7 10.3 %copy-start.9 = (bf16[12,32,512]{2,1,0:T(8,128)(2,1)}, bf16[12,32,512]{2,1,0:T(8,128)(2,1)S(1)}, u32[]{:S(2)}) copy-start(bf16[12,32,512]{2,1,0:T(8,128)(2,1)S(1)} %collective-permute-done.6.refs_7_) | copy-start | bytes 1179652
  71.7 10.2 %collective-permute-start.15 = (bf16[4,16,6144]{2,1,0:T(8,128)(2,1)S(1)}, bf16[4,16,6144]{2,1,0:T(8,128)(2,1)S(1)}, u32[]{:S(2)}, u32[]{:S(2)}) collective-permute-start(bf16[4,16,6144]{2,1,0:T(8,128)(2,1)S(1)} %collective-permute-done.10.refs_9_), channel_id=1, source_target_pairs={{0,1},{1,0},{2,3},{3,2},{4,5},{5,4},{6,7},{7,6},{8,9},{9,8},{10,11... | collective-permute-start | bytes 2359304 | tf_op jit(solution)/shard_map/ppermute | solution.py:434
  73.6 8.3 %copy-start.10 = (bf16[2,16,6144]{2,1,0:T(8,128)(2,1)}, bf16[2,16,6144]{2,1,0:T(8,128)(2,1)S(1)}, u32[]{:S(2)}) copy-start(bf16[2,16,6144]{2,1,0:T(8,128)(2,1)S(1)} %collective-permute-done.13.refs_12_) | copy-start | bytes 1179652
  73.6 7.0 %collective-permute-start.18 = (bf16[2,16,6144]{2,1,0:T(8,128)(2,1)S(1)}, bf16[2,16,6144]{2,1,0:T(8,128)(2,1)S(1)}, u32[]{:S(2)}, u32[]{:S(2)}) collective-permute-start(bf16[2,16,6144]{2,1,0:T(8,128)(2,1)S(1)} %collective-permute-done.13.refs_12_), channel_id=1, source_target_pairs={{0,1},{1,0},{2,3},{3,2},{4,5},{5,4},{6,7},{7,6},{8,9},{9,8},{10,11... | collective-permute-start | bytes 1179656 | tf_op jit(solution)/shard_map/ppermute | solution.py:434
  78.2 3.7 %copy-start.11 = (bf16[2,16,6144]{2,1,0:T(8,128)(2,1)}, bf16[2,16,6144]{2,1,0:T(8,128)(2,1)S(1)}, u32[]{:S(2)}) copy-start(bf16[2,16,6144]{2,1,0:T(8,128)(2,1)S(1)} %collective-permute-done.12.refs_11_) | copy-start | bytes 1179652
  78.2 3.7 %collective-permute-start.17 = (bf16[2,16,6144]{2,1,0:T(8,128)(2,1)S(1)}, bf16[2,16,6144]{2,1,0:T(8,128)(2,1)S(1)}, u32[]{:S(2)}, u32[]{:S(2)}) collective-permute-start(bf16[2,16,6144]{2,1,0:T(8,128)(2,1)S(1)} %collective-permute-done.12.refs_11_), channel_id=1, source_target_pairs={{0,1},{1,0},{2,3},{3,2},{4,5},{5,4},{6,7},{7,6},{8,9},{9,8},{10,11... | collective-permute-start | bytes 1179656 | tf_op jit(solution)/shard_map/ppermute | solution.py:434
  80.6 1.4 %copy-start.3 = (bf16[4,16,6144]{2,1,0:T(8,128)(2,1)}, bf16[4,16,6144]{2,1,0:T(8,128)(2,1)S(1)}, u32[]{:S(2)}) copy-start(bf16[4,16,6144]{2,1,0:T(8,128)(2,1)S(1)} %collective-permute-done.14.refs_13_) | copy-start | bytes 2359300
  80.6 1.4 %copy-start.12 = (bf16[2,16,6144]{2,1,0:T(8,128)(2,1)}, bf16[2,16,6144]{2,1,0:T(8,128)(2,1)S(1)}, u32[]{:S(2)}) copy-start(bf16[2,16,6144]{2,1,0:T(8,128)(2,1)S(1)} %collective-permute-done.18.refs_17_) | copy-start | bytes 1179652
  80.6 1.4 %copy-start.4 = (bf16[4,16,6144]{2,1,0:T(8,128)(2,1)}, bf16[4,16,6144]{2,1,0:T(8,128)(2,1)S(1)}, u32[]{:S(2)}) copy-start(bf16[4,16,6144]{2,1,0:T(8,128)(2,1)S(1)} %collective-permute-done.16.refs_15_) | copy-start | bytes 2359300
  81.9 1.0 %copy-start.5 = (bf16[4,16,6144]{2,1,0:T(8,128)(2,1)}, bf16[4,16,6144]{2,1,0:T(8,128)(2,1)S(1)}, u32[]{:S(2)}) copy-start(bf16[4,16,6144]{2,1,0:T(8,128)(2,1)S(1)} %collective-permute-done.15.refs_14_) | copy-start | bytes 2359300
  (3 other events, 2.2 us)

commit v4 on v3

--- a/solution.py
+++ b/solution.py
@@ -19,7 +19,7 @@
 EDGE = RIM * LEV
 STRIP = 32
 REGION = LINE + 2 * STRIP
-DIRECT = 80
+DIRECT = 64
 WIDE = LINE + 2 * EDGE
 SPREAD = WINS * LEV * SLOT
 FF = 2048

time: 104 us -> 104 us (level)
  starting transfers between devices: 66.6 us -> 60.3 us
  waiting for transfers between devices: 6.56 us -> 12.8 us
    ppermute x19, waiting for transfers between devices: 6.56 us -> 12.8 us  [send(): return lax.ppermute(value, AXES, pairs)]
    ppermute x19, starting transfers between devices: 66.6 us -> 60.3 us  [send(): return lax.ppermute(value, AXES, pairs)]
where the time goes in v4:
time: 104 us; the launch traced here: 103 us
  starting transfers between devices  60.3 us (58%)
  Pallas kernels  25.3 us (24%)
  waiting for transfers between devices  12.8 us (12%)
  local copies, waits for them, and re-layouts  2.64 us (3%)
  other arithmetic  1.13 us (1%)
    ppermute x19, starting transfers between devices, send(): return lax.ppermute(value, AXES, pairs)  60.3 us
    pallas_call x1, Pallas kernels, block_call(): pl.pallas_call(functools.partial(block_kernel, position), out_shape=jax.S...  19.8 us
    ppermute x19, waiting for transfers between devices, send(): return lax.ppermute(value, AXES, pairs)  12.8 us
    pallas_call x1, Pallas kernels, pack_call(): pl.pallas_call(functools.partial(pack_kernel, position), out_shape=[jax.S...  3.05 us
    unnamed x32, local copies, waits for them, and re-layouts  2.58 us
    pallas_call x1, Pallas kernels, edge_call(): pl.pallas_call(functools.partial(edge_kernel, position), out_shape=[jax.S...  2.49 us
  transfers between devices with their start and end apart: 19, of which 4 were waited for; matrix products, arithmetic and copies ran while one was open for 1% of the time, Pallas kernels for 2%

profile of v4, /device:TPU:1, one launch (start us, length us, event | category | flops | bytes accessed | tf_op | source)
XLA Modules:
  0.0 102.9 jit_solution(9888210715014728059)
XLA Ops:
  0.0 3.1 %pack.1 = (bf16[16,6144]{1,0:T(8,128)(2,1)}, bf16[3,144,512]{2,1,0:T(8,128)(2,1)}, bf16[3,144,512]{2,1,0:T(8,128)(2,1)}, bf16[3,64,512]{2,1,0:T(8,128)(2,1)}, bf16[3,80,512]{2,1,0:T(8,128)(2,1)}) custom-call(f32[1,512]{1,0:T(1,128)} %bitcast.14, bf16[6,36,4,512]{3,2,1,0:T(4,128)(2,1)} %bitcast.12, bf16[16,1536]{1,0:T(8,128)(2,1)} %qkv_ref.1, ...), custom_call_target="tpu_custom_call" | custom-call | tf_op jit(solution)/shard_map/pack/pallas_call | solution.py:78
  3.1 3.9 %collective-permute-start.9 = (bf16[16,6144]{1,0:T(8,128)(2,1)}, bf16[16,6144]{1,0:T(8,128)(2,1)S(1)}, u32[]{:S(2)}, u32[]{:S(2)}) collective-permute-start(bf16[16,6144]{1,0:T(8,128)(2,1)} %get-tuple-element.18), channel_id=1, source_target_pairs={{0,2},{1,9},{2,4},{3,11},{4,6},{5,13},{6,256},{7,15},{8,10},{9,17}... | collective-permute-start | bytes 589832 | tf_op jit(solution)/shard_map/ppermute | solution.py:434
  7.0 3.2 %collective-permute-start.8 = (bf16[16,6144]{1,0:T(8,128)(2,1)}, bf16[16,6144]{1,0:T(8,128)(2,1)S(1)}, u32[]{:S(2)}, u32[]{:S(2)}) collective-permute-start(bf16[16,6144]{1,0:T(8,128)(2,1)} %get-tuple-element.18), channel_id=1, source_target_pairs={{0,262},{1,25},{2,0},{3,27},{4,2},{5,29},{6,4},{7,31},{8,270},{9,1... | collective-permute-start | bytes 589832 | tf_op jit(solution)/shard_map/ppermute | solution.py:434
  10.2 3.6 %collective-permute-start.7 = (bf16[16,6144]{1,0:T(8,128)(2,1)}, bf16[16,6144]{1,0:T(8,128)(2,1)S(1)}, u32[]{:S(2)}, u32[]{:S(2)}) collective-permute-start(bf16[16,6144]{1,0:T(8,128)(2,1)} %get-tuple-element.18), channel_id=1, source_target_pairs={{0,4},{1,17},{2,262},{3,19},{4,256},{5,21},{6,2},{7,23},{8,12},{9,... | collective-permute-start | bytes 589832 | tf_op jit(solution)/shard_map/ppermute | solution.py:434
  13.8 0.7 collective-permute-start.2
  14.5 1.3 %collective-permute-start.3 = (bf16[3,80,512]{2,1,0:T(8,128)(2,1)}, bf16[3,80,512]{2,1,0:T(8,128)(2,1)S(1)}, u32[]{:S(2)}, u32[]{:S(2)}) collective-permute-start(bf16[3,80,512]{2,1,0:T(8,128)(2,1)} %get-tuple-element.15), channel_id=1, source_target_pairs={{224,0},{225,1},{226,2},{227,3},{228,4},{229,5},{230,6},{231,7},{2... | collective-permute-start | bytes 737288 | tf_op jit(solution)/shard_map/ppermute | solution.py:434
  15.9 1.3 %collective-permute-start.1 = (bf16[3,144,512]{2,1,0:T(8,128)(2,1)}, bf16[3,144,512]{2,1,0:T(8,128)(2,1)S(1)}, u32[]{:S(2)}, u32[]{:S(2)}) collective-permute-start(bf16[3,144,512]{2,1,0:T(8,128)(2,1)} %get-tuple-element.12.top_ref.refs_0_), channel_id=1, source_target_pairs={{32,0},{33,1},{34,2},{35,3},{36,4},{37,5},{38,6},{39,7},{40,8},{41... | collective-permute-start | bytes 1327112 | tf_op jit(solution)/shard_map/ppermute | solution.py:434
  17.2 4.0 %collective-permute-start = (bf16[3,144,512]{2,1,0:T(8,128)(2,1)}, bf16[3,144,512]{2,1,0:T(8,128)(2,1)S(1)}, u32[]{:S(2)}, u32[]{:S(2)}) collective-permute-start(bf16[3,144,512]{2,1,0:T(8,128)(2,1)} %get-tuple-element.13.low_ref.refs_1_), channel_id=1, source_target_pairs={{0,32},{1,33},{2,34},{3,35},{4,36},{5,37},{6,38},{7,39},{8,40},{9,... | collective-permute-start | bytes 1327112 | tf_op jit(solution)/shard_map/ppermute | solution.py:434
  21.2 1.0 select_bitcast_fusion.3
  22.3 9.0 %collective-permute-done.3 = bf16[3,80,512]{2,1,0:T(8,128)(2,1)S(1)} collective-permute-done((bf16[3,80,512]{2,1,0:T(8,128)(2,1)}, bf16[3,80,512]{2,1,0:T(8,128)(2,1)S(1)}, u32[]{:S(2)}, u32[]{:S(2)}) %collective-permute-start.3) | collective-permute-done | bytes 245792 | tf_op jit(solution)/shard_map/ppermute | solution.py:434
  31.2 8.0 %collective-permute-start.4 = (bf16[3,80,512]{2,1,0:T(8,128)(2,1)S(1)}, bf16[3,80,512]{2,1,0:T(8,128)(2,1)S(1)}, u32[]{:S(2)}, u32[]{:S(2)}) collective-permute-start(bf16[3,80,512]{2,1,0:T(8,128)(2,1)S(1)} %collective-permute-done.3), channel_id=1, source_target_pairs={{0,256},{1,257},{2,258},{3,259},{4,260},{5,261},{6,262},{7,263},{8... | collective-permute-start | bytes 737288 | tf_op jit(solution)/shard_map/ppermute | solution.py:434
  39.4 1.9 %collective-permute-start.11 = (bf16[4,16,6144]{2,1,0:T(8,128)(2,1)S(1)}, bf16[4,16,6144]{2,1,0:T(8,128)(2,1)S(1)}, u32[]{:S(2)}, u32[]{:S(2)}) collective-permute-start(bf16[4,16,6144]{2,1,0:T(8,128)(2,1)S(1)} %pad_maximum_fusion.refs_8_), channel_id=1, source_target_pairs={{0,24},{1,263},{2,26},{3,1},{4,28},{5,3},{6,30},{7,5},{8,0},{9,271... | collective-permute-start | bytes 2359304 | tf_op jit(solution)/shard_map/ppermute | solution.py:434
  41.3 3.4 %collective-permute-start.10 = (bf16[4,16,6144]{2,1,0:T(8,128)(2,1)S(1)}, bf16[4,16,6144]{2,1,0:T(8,128)(2,1)S(1)}, u32[]{:S(2)}, u32[]{:S(2)}) collective-permute-start(bf16[4,16,6144]{2,1,0:T(8,128)(2,1)S(1)} %pad_maximum_fusion.refs_8_), channel_id=1, source_target_pairs={{0,8},{1,3},{2,10},{3,5},{4,12},{5,7},{6,14},{7,257},{8,16},{9,11}... | collective-permute-start | bytes 2359304 | tf_op jit(solution)/shard_map/ppermute | solution.py:434
  44.8 0.7 copy-done.6
  45.5 0.1 copy-done.7
  45.6 0.7 copy-done.14
  46.3 2.5 %edges.1 = (bf16[12,32,512]{2,1,0:T(8,128)(2,1)}, bf16[12,32,512]{2,1,0:T(8,128)(2,1)}) custom-call(bf16[3,144,512]{2,1,0:T(8,128)(2,1)} %get-tuple-element.12.top_ref.refs_0_, bf16[3,144,512]{2,1,0:T(8,128)(2,1)} %get-tuple-element.13.low_ref.refs_1_, bf16[3,144,512]{2,1,0:T(8,128)(2,1)} %copy-done.7, bf16[3,144,512]{2,1,0:T(8,128)(2,1)} %copy-done.6, ...), custom_call_target="tpu_custom_call" | custom-call | flops 10000000000 | bytes 8388608 | tf_op jit(solution)/shard_map/edges/pallas_call | solution.py:146
  48.8 10.4 %collective-permute-start.5 = (bf16[12,32,512]{2,1,0:T(8,128)(2,1)}, bf16[12,32,512]{2,1,0:T(8,128)(2,1)S(1)}, u32[]{:S(2)}, u32[]{:S(2)}) collective-permute-start(bf16[12,32,512]{2,1,0:T(8,128)(2,1)} %get-tuple-element.16), channel_id=1, source_target_pairs={{0,1},{1,2},{2,3},{3,4},{4,5},{5,6},{6,7},{7,8},{8,9},{9,10},{10,1... | collective-permute-start | bytes 1179656 | tf_op jit(solution)/shard_map/ppermute | solution.py:434
  59.2 1.9 %collective-permute-start.6 = (bf16[12,32,512]{2,1,0:T(8,128)(2,1)}, bf16[12,32,512]{2,1,0:T(8,128)(2,1)S(1)}, u32[]{:S(2)}, u32[]{:S(2)}) collective-permute-start(bf16[12,32,512]{2,1,0:T(8,128)(2,1)} %get-tuple-element.17), channel_id=1, source_target_pairs={{0,31},{1,0},{2,1},{3,2},{4,3},{5,4},{6,5},{7,6},{8,7},{9,8},{10,9... | collective-permute-start | bytes 1179656 | tf_op jit(solution)/shard_map/ppermute | solution.py:434
  61.1 2.6 %collective-permute-start.14 = (bf16[4,16,6144]{2,1,0:T(8,128)(2,1)S(1)}, bf16[4,16,6144]{2,1,0:T(8,128)(2,1)S(1)}, u32[]{:S(2)}, u32[]{:S(2)}) collective-permute-start(bf16[4,16,6144]{2,1,0:T(8,128)(2,1)S(1)} %pad_maximum_fusion.refs_8_), channel_id=1, source_target_pairs={{0,1},{1,0},{2,3},{3,2},{4,5},{5,4},{6,7},{7,6},{8,9},{9,8},{10,11... | collective-permute-start | bytes 2359304 | tf_op jit(solution)/shard_map/ppermute | solution.py:434
  63.7 1.6 %collective-permute-done.11.refs_10_ = bf16[4,16,6144]{2,1,0:T(8,128)(2,1)S(1)} collective-permute-done((bf16[4,16,6144]{2,1,0:T(8,128)(2,1)S(1)}, bf16[4,16,6144]{2,1,0:T(8,128)(2,1)S(1)}, u32[]{:S(2)}, u32[]{:S(2)}) %collective-permute-start.11) | collective-permute-done | bytes 786464 | tf_op jit(solution)/shard_map/ppermute | solution.py:434
  65.4 2.6 %collective-permute-start.13 = (bf16[2,16,6144]{2,1,0:T(8,128)(2,1)S(1)}, bf16[2,16,6144]{2,1,0:T(8,128)(2,1)S(1)}, u32[]{:S(2)}, u32[]{:S(2)}) collective-permute-start(bf16[2,16,6144]{2,1,0:T(8,128)(2,1)S(1)} %slice.9), channel_id=1, source_target_pairs={{0,24},{1,263},{2,26},{3,1},{4,28},{5,3},{6,30},{7,5},{8,0},{9,271... | collective-permute-start | bytes 1179656 | tf_op jit(solution)/shard_map/ppermute | solution.py:434
  68.0 2.7 %collective-permute-start.12 = (bf16[2,16,6144]{2,1,0:T(8,128)(2,1)S(1)}, bf16[2,16,6144]{2,1,0:T(8,128)(2,1)S(1)}, u32[]{:S(2)}, u32[]{:S(2)}) collective-permute-start(bf16[2,16,6144]{2,1,0:T(8,128)(2,1)S(1)} %slice.8), channel_id=1, source_target_pairs={{0,8},{1,3},{2,10},{3,5},{4,12},{5,7},{6,14},{7,257},{8,16},{9,11}... | collective-permute-start | bytes 1179656 | tf_op jit(solution)/shard_map/ppermute | solution.py:434
  70.7 1.9 %collective-permute-start.16 = (bf16[4,16,6144]{2,1,0:T(8,128)(2,1)S(1)}, bf16[4,16,6144]{2,1,0:T(8,128)(2,1)S(1)}, u32[]{:S(2)}, u32[]{:S(2)}) collective-permute-start(bf16[4,16,6144]{2,1,0:T(8,128)(2,1)S(1)} %collective-permute-done.11.refs_10_), channel_id=1, source_target_pairs={{0,1},{1,0},{2,3},{3,2},{4,5},{5,4},{6,7},{7,6},{8,9},{9,8},{10,11... | collective-permute-start | bytes 2359304 | tf_op jit(solution)/shard_map/ppermute | solution.py:434
  72.7 2.4 %collective-permute-start.15 = (bf16[4,16,6144]{2,1,0:T(8,128)(2,1)S(1)}, bf16[4,16,6144]{2,1,0:T(8,128)(2,1)S(1)}, u32[]{:S(2)}, u32[]{:S(2)}) collective-permute-start(bf16[4,16,6144]{2,1,0:T(8,128)(2,1)S(1)} %collective-permute-done.10.refs_9_), channel_id=1, source_target_pairs={{0,1},{1,0},{2,3},{3,2},{4,5},{5,4},{6,7},{7,6},{8,9},{9,8},{10,11... | collective-permute-start | bytes 2359304 | tf_op jit(solution)/shard_map/ppermute | solution.py:434
  75.1 1.9 %collective-permute-start.18 = (bf16[2,16,6144]{2,1,0:T(8,128)(2,1)S(1)}, bf16[2,16,6144]{2,1,0:T(8,128)(2,1)S(1)}, u32[]{:S(2)}, u32[]{:S(2)}) collective-permute-start(bf16[2,16,6144]{2,1,0:T(8,128)(2,1)S(1)} %collective-permute-done.13.refs_12_), channel_id=1, source_target_pairs={{0,1},{1,0},{2,3},{3,2},{4,5},{5,4},{6,7},{7,6},{8,9},{9,8},{10,11... | collective-permute-start | bytes 1179656 | tf_op jit(solution)/shard_map/ppermute | solution.py:434
  77.1 1.0 collective-permute-done.12.refs_11_
  78.0 2.5 %collective-permute-start.17 = (bf16[2,16,6144]{2,1,0:T(8,128)(2,1)S(1)}, bf16[2,16,6144]{2,1,0:T(8,128)(2,1)S(1)}, u32[]{:S(2)}, u32[]{:S(2)}) collective-permute-start(bf16[2,16,6144]{2,1,0:T(8,128)(2,1)S(1)} %collective-permute-done.12.refs_11_), channel_id=1, source_target_pairs={{0,1},{1,0},{2,3},{3,2},{4,5},{5,4},{6,7},{7,6},{8,9},{9,8},{10,11... | collective-permute-start | bytes 1179656 | tf_op jit(solution)/shard_map/ppermute | solution.py:434
  80.6 1.3 %collective-permute-done.17.refs_16_ = bf16[2,16,6144]{2,1,0:T(8,128)(2,1)S(1)} collective-permute-done((bf16[2,16,6144]{2,1,0:T(8,128)(2,1)S(1)}, bf16[2,16,6144]{2,1,0:T(8,128)(2,1)S(1)}, u32[]{:S(2)}, u32[]{:S(2)}) %collective-permute-start.17) | collective-permute-done | bytes 393248 | tf_op jit(solution)/shard_map/ppermute | solution.py:434
  82.0 0.7 copy-done.13
  82.7 0.3 copy-done.5
  82.9 19.8 %block.1 = bf16[6,36,4,512]{3,2,1,0:T(4,128)(2,1)} custom-call(f32[1,512]{1,0:T(1,128)} %bitcast.15, bf16[6,36,4,512]{3,2,1,0:T(4,128)(2,1)} %bitcast.13, bf16[3,144,512]{2,1,0:T(8,128)(2,1)} %get-tuple-element.12.top_ref.refs_0_, bf16[3,144,512]{2,1,0:T(8,128)(2,1)} %get-tuple-element.13.low_ref.refs_1_, bf16[3,144,512]{2,1,0:T(8,128)(2,1)} %copy-done.7, ...), custom_call_target="tpu_custom_call" | custom-call | tf_op jit(solution)/shard_map/block/pallas_call | solution.py:338
  (45 shorter events, 0.2 us)
Async XLA Ops:
  3.1 12.8 %collective-permute-start.9 = (bf16[16,6144]{1,0:T(8,128)(2,1)}, bf16[16,6144]{1,0:T(8,128)(2,1)S(1)}, u32[]{:S(2)}, u32[]{:S(2)}) collective-permute-start(bf16[16,6144]{1,0:T(8,128)(2,1)} %get-tuple-element.18), channel_id=1, source_target_pairs={{0,2},{1,9},{2,4},{3,11},{4,6},{5,13},{6,256},{7,15},{8,10},{9,17}... | collective-permute-start | bytes 589832 | tf_op jit(solution)/shard_map/ppermute | solution.py:434
  7.0 10.2 %collective-permute-start.8 = (bf16[16,6144]{1,0:T(8,128)(2,1)}, bf16[16,6144]{1,0:T(8,128)(2,1)S(1)}, u32[]{:S(2)}, u32[]{:S(2)}) collective-permute-start(bf16[16,6144]{1,0:T(8,128)(2,1)} %get-tuple-element.18), channel_id=1, source_target_pairs={{0,262},{1,25},{2,0},{3,27},{4,2},{5,29},{6,4},{7,31},{8,270},{9,1... | collective-permute-start | bytes 589832 | tf_op jit(solution)/shard_map/ppermute | solution.py:434
  10.2 11.0 %collective-permute-start.7 = (bf16[16,6144]{1,0:T(8,128)(2,1)}, bf16[16,6144]{1,0:T(8,128)(2,1)S(1)}, u32[]{:S(2)}, u32[]{:S(2)}) collective-permute-start(bf16[16,6144]{1,0:T(8,128)(2,1)} %get-tuple-element.18), channel_id=1, source_target_pairs={{0,4},{1,17},{2,262},{3,19},{4,256},{5,21},{6,2},{7,23},{8,12},{9,... | collective-permute-start | bytes 589832 | tf_op jit(solution)/shard_map/ppermute | solution.py:434
  13.8 27.5 %collective-permute-start.2 = (bf16[3,64,512]{2,1,0:T(8,128)(2,1)}, bf16[3,64,512]{2,1,0:T(8,128)(2,1)S(1)}, u32[]{:S(2)}, u32[]{:S(2)}) collective-permute-start(bf16[3,64,512]{2,1,0:T(8,128)(2,1)} %get-tuple-element.14), channel_id=1, source_target_pairs={{224,256},{225,257},{226,258},{227,259},{228,260},{229,261},{230,2... | collective-permute-start | bytes 589832 | tf_op jit(solution)/shard_map/ppermute | solution.py:434
  14.5 16.7 %collective-permute-start.3 = (bf16[3,80,512]{2,1,0:T(8,128)(2,1)}, bf16[3,80,512]{2,1,0:T(8,128)(2,1)S(1)}, u32[]{:S(2)}, u32[]{:S(2)}) collective-permute-start(bf16[3,80,512]{2,1,0:T(8,128)(2,1)} %get-tuple-element.15), channel_id=1, source_target_pairs={{224,0},{225,1},{226,2},{227,3},{228,4},{229,5},{230,6},{231,7},{2... | collective-permute-start | bytes 737288 | tf_op jit(solution)/shard_map/ppermute | solution.py:434
  15.9 28.8 %collective-permute-start.1 = (bf16[3,144,512]{2,1,0:T(8,128)(2,1)}, bf16[3,144,512]{2,1,0:T(8,128)(2,1)S(1)}, u32[]{:S(2)}, u32[]{:S(2)}) collective-permute-start(bf16[3,144,512]{2,1,0:T(8,128)(2,1)} %get-tuple-element.12.top_ref.refs_0_), channel_id=1, source_target_pairs={{32,0},{33,1},{34,2},{35,3},{36,4},{37,5},{38,6},{39,7},{40,8},{41... | collective-permute-start | bytes 1327112 | tf_op jit(solution)/shard_map/ppermute | solution.py:434
  17.2 27.6 %collective-permute-start = (bf16[3,144,512]{2,1,0:T(8,128)(2,1)}, bf16[3,144,512]{2,1,0:T(8,128)(2,1)S(1)}, u32[]{:S(2)}, u32[]{:S(2)}) collective-permute-start(bf16[3,144,512]{2,1,0:T(8,128)(2,1)} %get-tuple-element.13.low_ref.refs_1_), channel_id=1, source_target_pairs={{0,32},{1,33},{2,34},{3,35},{4,36},{5,37},{6,38},{7,39},{8,40},{9,... | collective-permute-start | bytes 1327112 | tf_op jit(solution)/shard_map/ppermute | solution.py:434
  31.2 13.5 %collective-permute-start.4 = (bf16[3,80,512]{2,1,0:T(8,128)(2,1)S(1)}, bf16[3,80,512]{2,1,0:T(8,128)(2,1)S(1)}, u32[]{:S(2)}, u32[]{:S(2)}) collective-permute-start(bf16[3,80,512]{2,1,0:T(8,128)(2,1)S(1)} %collective-permute-done.3), channel_id=1, source_target_pairs={{0,256},{1,257},{2,258},{3,259},{4,260},{5,261},{6,262},{7,263},{8... | collective-permute-start | bytes 737288 | tf_op jit(solution)/shard_map/ppermute | solution.py:434
  39.4 21.7 %copy-start = (bf16[4,16,6144]{2,1,0:T(8,128)(2,1)}, bf16[4,16,6144]{2,1,0:T(8,128)(2,1)S(1)}, u32[]{:S(2)}) copy-start(bf16[4,16,6144]{2,1,0:T(8,128)(2,1)S(1)} %pad_maximum_fusion.refs_8_) | copy-start | bytes 2359300
  39.4 25.9 %collective-permute-start.11 = (bf16[4,16,6144]{2,1,0:T(8,128)(2,1)S(1)}, bf16[4,16,6144]{2,1,0:T(8,128)(2,1)S(1)}, u32[]{:S(2)}, u32[]{:S(2)}) collective-permute-start(bf16[4,16,6144]{2,1,0:T(8,128)(2,1)S(1)} %pad_maximum_fusion.refs_8_), channel_id=1, source_target_pairs={{0,24},{1,263},{2,26},{3,1},{4,28},{5,3},{6,30},{7,5},{8,0},{9,271... | collective-permute-start | bytes 2359304 | tf_op jit(solution)/shard_map/ppermute | solution.py:434
  41.3 3.4 %copy-start.15 = (bf16[3,64,512]{2,1,0:T(8,128)(2,1)}, bf16[3,64,512]{2,1,0:T(8,128)(2,1)S(1)}, u32[]{:S(2)}) copy-start(bf16[3,64,512]{2,1,0:T(8,128)(2,1)S(1)} %collective-permute-done.2.direct_ref.refs_4_) | copy-start | bytes 589828
  41.3 26.6 %collective-permute-start.10 = (bf16[4,16,6144]{2,1,0:T(8,128)(2,1)S(1)}, bf16[4,16,6144]{2,1,0:T(8,128)(2,1)S(1)}, u32[]{:S(2)}, u32[]{:S(2)}) collective-permute-start(bf16[4,16,6144]{2,1,0:T(8,128)(2,1)S(1)} %pad_maximum_fusion.refs_8_), channel_id=1, source_target_pairs={{0,8},{1,3},{2,10},{3,5},{4,12},{5,7},{6,14},{7,257},{8,16},{9,11}... | collective-permute-start | bytes 2359304 | tf_op jit(solution)/shard_map/ppermute | solution.py:434
  44.7 0.9 copy-start.7
  48.8 21.9 %collective-permute-start.5 = (bf16[12,32,512]{2,1,0:T(8,128)(2,1)}, bf16[12,32,512]{2,1,0:T(8,128)(2,1)S(1)}, u32[]{:S(2)}, u32[]{:S(2)}) collective-permute-start(bf16[12,32,512]{2,1,0:T(8,128)(2,1)} %get-tuple-element.16), channel_id=1, source_target_pairs={{0,1},{1,2},{2,3},{3,4},{4,5},{5,6},{6,7},{7,8},{8,9},{9,10},{10,1... | collective-permute-start | bytes 1179656 | tf_op jit(solution)/shard_map/ppermute | solution.py:434
  59.2 13.5 %collective-permute-start.6 = (bf16[12,32,512]{2,1,0:T(8,128)(2,1)}, bf16[12,32,512]{2,1,0:T(8,128)(2,1)S(1)}, u32[]{:S(2)}, u32[]{:S(2)}) collective-permute-start(bf16[12,32,512]{2,1,0:T(8,128)(2,1)} %get-tuple-element.17), channel_id=1, source_target_pairs={{0,31},{1,0},{2,1},{3,2},{4,3},{5,4},{6,5},{7,6},{8,7},{9,8},{10,9... | collective-permute-start | bytes 1179656 | tf_op jit(solution)/shard_map/ppermute | solution.py:434
  61.1 19.4 %collective-permute-start.14 = (bf16[4,16,6144]{2,1,0:T(8,128)(2,1)S(1)}, bf16[4,16,6144]{2,1,0:T(8,128)(2,1)S(1)}, u32[]{:S(2)}, u32[]{:S(2)}) collective-permute-start(bf16[4,16,6144]{2,1,0:T(8,128)(2,1)S(1)} %pad_maximum_fusion.refs_8_), channel_id=1, source_target_pairs={{0,1},{1,0},{2,3},{3,2},{4,5},{5,4},{6,7},{7,6},{8,9},{9,8},{10,11... | collective-permute-start | bytes 2359304 | tf_op jit(solution)/shard_map/ppermute | solution.py:434
  65.3 5.4 %copy-start.1 = (bf16[4,16,6144]{2,1,0:T(8,128)(2,1)}, bf16[4,16,6144]{2,1,0:T(8,128)(2,1)S(1)}, u32[]{:S(2)}) copy-start(bf16[4,16,6144]{2,1,0:T(8,128)(2,1)S(1)} %collective-permute-done.11.refs_10_) | copy-start | bytes 2359300
  65.4 9.8 %collective-permute-start.13 = (bf16[2,16,6144]{2,1,0:T(8,128)(2,1)S(1)}, bf16[2,16,6144]{2,1,0:T(8,128)(2,1)S(1)}, u32[]{:S(2)}, u32[]{:S(2)}) collective-permute-start(bf16[2,16,6144]{2,1,0:T(8,128)(2,1)S(1)} %slice.9), channel_id=1, source_target_pairs={{0,24},{1,263},{2,26},{3,1},{4,28},{5,3},{6,30},{7,5},{8,0},{9,271... | collective-permute-start | bytes 1179656 | tf_op jit(solution)/shard_map/ppermute | solution.py:434
  68.0 13.9 %copy-start.2 = (bf16[4,16,6144]{2,1,0:T(8,128)(2,1)}, bf16[4,16,6144]{2,1,0:T(8,128)(2,1)S(1)}, u32[]{:S(2)}) copy-start(bf16[4,16,6144]{2,1,0:T(8,128)(2,1)S(1)} %collective-permute-done.10.refs_9_) | copy-start | bytes 2359300
  68.0 10.0 %collective-permute-start.12 = (bf16[2,16,6144]{2,1,0:T(8,128)(2,1)S(1)}, bf16[2,16,6144]{2,1,0:T(8,128)(2,1)S(1)}, u32[]{:S(2)}, u32[]{:S(2)}) collective-permute-start(bf16[2,16,6144]{2,1,0:T(8,128)(2,1)S(1)} %slice.8), channel_id=1, source_target_pairs={{0,8},{1,3},{2,10},{3,5},{4,12},{5,7},{6,14},{7,257},{8,16},{9,11}... | collective-permute-start | bytes 1179656 | tf_op jit(solution)/shard_map/ppermute | solution.py:434
  70.7 11.2 %copy-start.8 = (bf16[12,32,512]{2,1,0:T(8,128)(2,1)}, bf16[12,32,512]{2,1,0:T(8,128)(2,1)S(1)}, u32[]{:S(2)}) copy-start(bf16[12,32,512]{2,1,0:T(8,128)(2,1)S(1)} %collective-permute-done.5.refs_6_) | copy-start | bytes 1179652
  70.7 9.9 %collective-permute-start.16 = (bf16[4,16,6144]{2,1,0:T(8,128)(2,1)S(1)}, bf16[4,16,6144]{2,1,0:T(8,128)(2,1)S(1)}, u32[]{:S(2)}, u32[]{:S(2)}) collective-permute-start(bf16[4,16,6144]{2,1,0:T(8,128)(2,1)S(1)} %collective-permute-done.11.refs_10_), channel_id=1, source_target_pairs={{0,1},{1,0},{2,3},{3,2},{4,5},{5,4},{6,7},{7,6},{8,9},{9,8},{10,11... | collective-permute-start | bytes 2359304 | tf_op jit(solution)/shard_map/ppermute | solution.py:434
  72.7 9.2 %copy-start.9 = (bf16[12,32,512]{2,1,0:T(8,128)(2,1)}, bf16[12,32,512]{2,1,0:T(8,128)(2,1)S(1)}, u32[]{:S(2)}) copy-start(bf16[12,32,512]{2,1,0:T(8,128)(2,1)S(1)} %collective-permute-done.6.refs_7_) | copy-start | bytes 1179652
  72.7 9.2 %collective-permute-start.15 = (bf16[4,16,6144]{2,1,0:T(8,128)(2,1)S(1)}, bf16[4,16,6144]{2,1,0:T(8,128)(2,1)S(1)}, u32[]{:S(2)}, u32[]{:S(2)}) collective-permute-start(bf16[4,16,6144]{2,1,0:T(8,128)(2,1)S(1)} %collective-permute-done.10.refs_9_), channel_id=1, source_target_pairs={{0,1},{1,0},{2,3},{3,2},{4,5},{5,4},{6,7},{7,6},{8,9},{9,8},{10,11... | collective-permute-start | bytes 2359304 | tf_op jit(solution)/shard_map/ppermute | solution.py:434
  75.1 6.8 %copy-start.10 = (bf16[2,16,6144]{2,1,0:T(8,128)(2,1)}, bf16[2,16,6144]{2,1,0:T(8,128)(2,1)S(1)}, u32[]{:S(2)}) copy-start(bf16[2,16,6144]{2,1,0:T(8,128)(2,1)S(1)} %collective-permute-done.13.refs_12_) | copy-start | bytes 1179652
  75.1 5.5 %collective-permute-start.18 = (bf16[2,16,6144]{2,1,0:T(8,128)(2,1)S(1)}, bf16[2,16,6144]{2,1,0:T(8,128)(2,1)S(1)}, u32[]{:S(2)}, u32[]{:S(2)}) collective-permute-start(bf16[2,16,6144]{2,1,0:T(8,128)(2,1)S(1)} %collective-permute-done.13.refs_12_), channel_id=1, source_target_pairs={{0,1},{1,0},{2,3},{3,2},{4,5},{5,4},{6,7},{7,6},{8,9},{9,8},{10,11... | collective-permute-start | bytes 1179656 | tf_op jit(solution)/shard_map/ppermute | solution.py:434
  78.0 3.9 %copy-start.11 = (bf16[2,16,6144]{2,1,0:T(8,128)(2,1)}, bf16[2,16,6144]{2,1,0:T(8,128)(2,1)S(1)}, u32[]{:S(2)}) copy-start(bf16[2,16,6144]{2,1,0:T(8,128)(2,1)S(1)} %collective-permute-done.12.refs_11_) | copy-start | bytes 1179652
  78.0 3.9 %collective-permute-start.17 = (bf16[2,16,6144]{2,1,0:T(8,128)(2,1)S(1)}, bf16[2,16,6144]{2,1,0:T(8,128)(2,1)S(1)}, u32[]{:S(2)}, u32[]{:S(2)}) collective-permute-start(bf16[2,16,6144]{2,1,0:T(8,128)(2,1)S(1)} %collective-permute-done.12.refs_11_), channel_id=1, source_target_pairs={{0,1},{1,0},{2,3},{3,2},{4,5},{5,4},{6,7},{7,6},{8,9},{9,8},{10,11... | collective-permute-start | bytes 1179656 | tf_op jit(solution)/shard_map/ppermute | solution.py:434
  80.6 1.4 %copy-start.3 = (bf16[4,16,6144]{2,1,0:T(8,128)(2,1)}, bf16[4,16,6144]{2,1,0:T(8,128)(2,1)S(1)}, u32[]{:S(2)}) copy-start(bf16[4,16,6144]{2,1,0:T(8,128)(2,1)S(1)} %collective-permute-done.14.refs_13_) | copy-start | bytes 2359300
  80.6 1.4 %copy-start.12 = (bf16[2,16,6144]{2,1,0:T(8,128)(2,1)}, bf16[2,16,6144]{2,1,0:T(8,128)(2,1)S(1)}, u32[]{:S(2)}) copy-start(bf16[2,16,6144]{2,1,0:T(8,128)(2,1)S(1)} %collective-permute-done.18.refs_17_) | copy-start | bytes 1179652
  80.6 1.4 %copy-start.4 = (bf16[4,16,6144]{2,1,0:T(8,128)(2,1)}, bf16[4,16,6144]{2,1,0:T(8,128)(2,1)S(1)}, u32[]{:S(2)}) copy-start(bf16[4,16,6144]{2,1,0:T(8,128)(2,1)S(1)} %collective-permute-done.16.refs_15_) | copy-start | bytes 2359300
  81.9 1.0 %copy-start.5 = (bf16[4,16,6144]{2,1,0:T(8,128)(2,1)}, bf16[4,16,6144]{2,1,0:T(8,128)(2,1)S(1)}, u32[]{:S(2)}) copy-start(bf16[4,16,6144]{2,1,0:T(8,128)(2,1)S(1)} %collective-permute-done.15.refs_14_) | copy-start | bytes 2359300
  (3 other events, 2.3 us)
